TPU v7x, 512 devices: a whole 4x8x8 slice. The times are simulated.
512 devices in a mesh: pipe: 32 (over x, y), expert: 16 (over z, core).
Axes of the slice: x: 4, y: 8, z: 8, core: 2. Of those that a mesh axis runs over, the one named last changes fastest.
Arguments:
- first_state: bfloat16 [32, 512, 3584], P('pipe', 'expert'), may hold values from -6 to 6
- second_state: bfloat16 [32, 512, 3584], P('pipe', 'expert'), may hold values from -6 to 6
- first_enter: bfloat16 [1, 512, 3584], P(None, 'expert'), may hold values from -6 to 6
- second_enter: bfloat16 [1, 512, 3584], P(None, 'expert'), may hold values from -6 to 6
- norm_gain: float32 [32, 3584], P('pipe'), may hold values from 0.5 to 1.5
- router: float32 [32, 3584, 2], P('pipe'), may hold values from -0.09375 to 0.09375
- gate_proj: bfloat16 [32, 3584, 2048], P('pipe', None, 'expert'), may hold values from -0.09375 to 0.09375
- up_proj: bfloat16 [32, 3584, 2048], P('pipe', None, 'expert'), may hold values from -0.09375 to 0.09375
- down_proj: bfloat16 [32, 2048, 3584], P('pipe', 'expert'), may hold values from -0.1875 to 0.1875
- first_routes: int32 [2, 32, 512, 1], P(None, 'pipe', 'expert'), may hold values from 0 to 1; in each aligned block of 32 rows (0 to 31, 32 to 63, ..., all dimensions but the last counted through in order) at most 17 rows name the same one
- second_routes: int32 [2, 32, 512, 1], P(None, 'pipe', 'expert'), may hold values from 0 to 1; in each aligned block of 32 rows (0 to 31, 32 to 63, ..., all dimensions but the last counted through in order) at most 17 rows name the same one
Outputs:
- first_out: bfloat16 [2, 32, 512, 3584], P(None, 'pipe', 'expert')
- second_out: bfloat16 [2, 32, 512, 3584], P(None, 'pipe', 'expert')
Inputs may be any that keep to these rules, and one draw needn't show every extreme that they name: `first_routes`: within the 32 rows of one device at one step and section no expert is named by more than 17 rows, a bound that some block reaches. `second_routes`: within the 32 rows of one device at one step and section no expert is named by more than 17 rows, a bound that some block reaches.
All inputs are finite; a program needn't handle non-finite values.
Results may differ from a plain program's by a relative error of at most 0.0067.
Values may be sent and summed in bfloat16 or wider, within the bound.
A program may use at most 64 MiB of HBM per device.

v0:
```python
from functools import partial

import jax
import jax.numpy as jnp
from jax import lax
from jax.sharding import PartitionSpec as P

EXP_WIN = 2
CAP = 17


epsilon = 1e-06
route_scale = 2.5


def passed_along(block, axis, distance):
    devices = range(lax.axis_size(axis))
    route = [(i - distance, i) for i in devices if i - distance in devices]
    return lax.ppermute(block, axis, route)


def normalize(tokens, gains):
    widened = tokens.astype(jnp.float32)
    inverse = lax.rsqrt(jnp.mean(widened * widened, axis=-1, keepdims=True) + epsilon)
    return (widened * inverse * gains[None, :]).astype(jnp.bfloat16)


def pack_tokens(tokens, gains, router, route):
    normed = normalize(tokens, gains)
    scores = jnp.dot(normed.astype(jnp.float32), router, precision=lax.Precision.HIGHEST)
    chosen = route[:, 0]
    onehot = (chosen[:, None] == jnp.arange(EXP_WIN, dtype=jnp.int32)[None, :]).astype(jnp.float32)
    weight = route_scale * jax.nn.sigmoid(jnp.sum(scores * onehot, axis=1))
    before = jnp.cumsum(onehot, axis=0) - onehot
    slots = jnp.sum(before * onehot, axis=1).astype(jnp.int32)
    tables = (
        (chosen[None, None, :] == jnp.arange(EXP_WIN, dtype=jnp.int32)[:, None, None])
        & (slots[None, None, :] == jnp.arange(CAP, dtype=jnp.int32)[None, :, None])
    ).astype(jnp.bfloat16)
    packed = jnp.einsum("gct,td->gcd", tables, normed, preferred_element_type=jnp.float32).astype(
        jnp.bfloat16
    )
    return (packed, tables, weight)


def expert_rows(received, gate_proj, up_proj, down_proj):
    flat_rows = received.reshape(-1, received.shape[-1])
    gate_act = jnp.dot(flat_rows, gate_proj, preferred_element_type=jnp.float32)
    up_act = jnp.dot(flat_rows, up_proj, preferred_element_type=jnp.float32)
    hidden = (jax.nn.silu(gate_act) * up_act).astype(jnp.bfloat16)
    part_sum = jnp.dot(hidden, down_proj, preferred_element_type=jnp.float32).astype(jnp.bfloat16)
    return lax.all_to_all(
        part_sum.reshape(received.shape), "expert", split_axis=0, concat_axis=0, tiled=True
    )


def expert_layer(blocks, routes, gains, router, gate_proj, up_proj, down_proj):
    packs = [pack_tokens(tokens, gains, router, route) for tokens, route in zip(blocks, routes)]
    packed = jnp.concatenate([entry[0] for entry in packs], axis=1)
    group_size = lax.axis_size("expert") // EXP_WIN
    worker = partial(expert_rows, gate_proj=gate_proj, up_proj=up_proj, down_proj=down_proj)
    outgoing = jnp.broadcast_to(packed[:, None], (EXP_WIN, group_size) + packed.shape[1:])
    outgoing = outgoing.reshape((-1,) + packed.shape[1:])
    returned = worker(lax.all_to_all(outgoing, "expert", split_axis=0, concat_axis=0, tiled=True))
    summed = jnp.sum(
        returned.reshape((EXP_WIN, group_size) + packed.shape[1:]).astype(jnp.float32), axis=1
    )
    results = []
    for member, (tokens, entry) in enumerate(zip(blocks, packs)):
        expert_out = jnp.einsum(
            "gct,gcd->td", entry[1].astype(jnp.float32), summed, precision=lax.Precision.HIGHEST
        )
        results.append(
            (tokens.astype(jnp.float32) + entry[2][:, None] * expert_out).astype(jnp.bfloat16)
        )
    return results


def shards(
    first_state,
    second_state,
    first_enter,
    second_enter,
    norm_gain,
    router,
    gate_proj,
    up_proj,
    down_proj,
    first_routes,
    second_routes,
):
    gains = norm_gain[0]
    router_cols = router[0]
    gate_local = gate_proj[0]
    up_local = up_proj[0]
    down_local = down_proj[0]
    position = lax.axis_index("pipe")
    final_section = lax.axis_size("pipe") - 1
    first_now = first_state[0]
    second_now = second_state[0]
    first_list = []
    second_list = []
    for step_index in range(first_routes.shape[0]):
        if step_index > 0:
            first_moved = passed_along(first_list[-1], "pipe", 1)
            second_moved = passed_along(second_list[-1], "pipe", -1)
            first_now = jnp.where(position == 0, first_enter[step_index - 1], first_moved)
            second_now = jnp.where(
                position == final_section, second_enter[step_index - 1], second_moved
            )
        first_route = first_routes[step_index, 0]
        second_route = second_routes[step_index, 0]
        first_done = expert_layer(
            [first_now], [first_route], gains, router_cols, gate_local, up_local, down_local
        )[0]
        second_done = expert_layer(
            [second_now], [second_route], gains, router_cols, gate_local, up_local, down_local
        )[0]
        first_list.append(first_done)
        second_list.append(second_done)
    first_out = jnp.stack(first_list)[:, None]
    second_out = jnp.stack(second_list)[:, None]
    return (first_out, second_out)


def solution(mesh):
    return jax.shard_map(
        shards,
        mesh=mesh,
        in_specs=(
            P("pipe", "expert", None),
            P("pipe", "expert", None),
            P(None, "expert", None),
            P(None, "expert", None),
            P("pipe", None),
            P("pipe", None, None),
            P("pipe", None, "expert"),
            P("pipe", None, "expert"),
            P("pipe", "expert", None),
            P(None, "pipe", "expert", None),
            P(None, "pipe", "expert", None),
        ),
        out_specs=(P(None, "pipe", "expert", None), P(None, "pipe", "expert", None)),
        check_vma=False,
    )
```

profile of v0, /device:TPU:6, one launch (start us, length us, event | category | flops | bytes accessed | tf_op | source)
XLA Modules:
  0.0 566.1 jit_solution(9644266119191929179)
XLA Ops:
  0.6 0.8 slice_bitcast_fusion
  1.4 1.1 fusion.51
  2.8 0.8 reduce
  3.6 1.2 convolution_convert_fusion.5
  4.8 1.8 broadcast_in_dim.15
  6.6 10.6 %all-to-all-start.4 = ((bf16[16,17,3584]{2,1,0:T(8,128)(2,1)}), bf16[16,17,3584]{2,1,0:T(8,128)(2,1)}, u32[]{:S(2)}, u32[]{:S(2)}) async-start(bf16[16,17,3584]{2,1,0:T(8,128)(2,1)} %bitcast.185), calls=%async_computation.4 | async-start | bytes 5505024 | tf_op jit(solution)/shard_map/all_to_all | solution.py:64
  17.2 0.5 slice_bitcast_fusion.2
  18.2 0.3 convolution_convert_fusion.7
  18.5 62.0 %all-to-all-done.4 = bf16[16,17,3584]{2,1,0:T(8,128)(2,1)} async-done(((bf16[16,17,3584]{2,1,0:T(8,128)(2,1)}), bf16[16,17,3584]{2,1,0:T(8,128)(2,1)}, u32[]{:S(2)}, u32[]{:S(2)}) %all-to-all-start.4) | async-done | bytes 1949728 | tf_op jit(solution)/shard_map/all_to_all | solution.py:64
  80.6 1.8 broadcast_in_dim.12
  82.3 4.7 all-to-all-start
  87.1 2.1 reshape.359
  89.2 1.8 fusion.36
  91.1 4.7 convolution_convert_fusion.1
  95.8 3.1 reshape.360
  98.9 51.5 %all-to-all-done = bf16[16,17,3584]{2,1,0:T(8,128)(2,1)} async-done(((bf16[16,17,3584]{2,1,0:T(8,128)(2,1)}), bf16[16,17,3584]{2,1,0:T(8,128)(2,1)}, u32[]{:S(2)}, u32[]{:S(2)}) %all-to-all-start) | async-done | bytes 1949728 | tf_op jit(solution)/shard_map/all_to_all | solution.py:64
  150.5 4.7 all-to-all-start.5
  155.2 2.1 reshape.353
  157.3 1.8 fusion.40
  159.2 4.7 convolution_convert_fusion.3
  163.9 3.1 reshape.354
  167.0 51.6 %all-to-all-done.5 = bf16[16,17,3584]{2,1,0:T(8,128)(2,1)} async-done(((bf16[16,17,3584]{2,1,0:T(8,128)(2,1)}), bf16[16,17,3584]{2,1,0:T(8,128)(2,1)}, u32[]{:S(2)}, u32[]{:S(2)}) %all-to-all-start.5) | async-done | bytes 1949728 | tf_op jit(solution)/shard_map/all_to_all | solution.py:52
  218.6 4.7 all-to-all-start.1
  223.5 0.4 fusion.20
  224.0 2.4 convert_reduce_fusion.1
  226.3 0.4 fusion.10
  226.7 5.7 collective-permute-start.1
  232.5 5.3 collective-permute-done.1
  237.8 0.2 fusion.59
  238.0 0.3 convolution_convert_fusion.4
  238.3 48.4 %all-to-all-done.1 = bf16[16,17,3584]{2,1,0:T(8,128)(2,1)} async-done(((bf16[16,17,3584]{2,1,0:T(8,128)(2,1)}), bf16[16,17,3584]{2,1,0:T(8,128)(2,1)}, u32[]{:S(2)}, u32[]{:S(2)}) %all-to-all-start.1) | async-done | bytes 1949728 | tf_op jit(solution)/shard_map/all_to_all | solution.py:52
  286.7 1.7 broadcast_in_dim.16
  288.4 4.7 all-to-all-start.6
  293.4 0.4 fusion.18
  293.8 2.3 convert_reduce_fusion.3
  296.2 0.4 fusion.8
  296.6 3.7 collective-permute-start
  300.4 8.1 %collective-permute-done = bf16[32,3584]{1,0:T(8,128)(2,1)S(1)} collective-permute-done((bf16[32,3584]{1,0:T(8,128)(2,1)S(1)}, bf16[32,3584]{1,0:T(8,128)(2,1)S(1)}, u32[]{:S(2)}, u32[]{:S(2)}) %collective-permute-start) | collective-permute-done | bytes 229408 | tf_op jit(solution)/shard_map/ppermute | solution.py:19
  308.5 0.2 fusion.56
  308.7 0.3 convolution_convert_fusion.6
  309.0 47.5 %all-to-all-done.6 = bf16[16,17,3584]{2,1,0:T(8,128)(2,1)} async-done(((bf16[16,17,3584]{2,1,0:T(8,128)(2,1)}), bf16[16,17,3584]{2,1,0:T(8,128)(2,1)}, u32[]{:S(2)}, u32[]{:S(2)}) %all-to-all-start.6) | async-done | bytes 1949728 | tf_op jit(solution)/shard_map/all_to_all | solution.py:64
  356.5 1.8 broadcast_in_dim.13
  358.3 4.7 all-to-all-start.2
  363.0 2.1 reshape.362
  365.1 2.5 fusion.34
  367.6 4.7 convolution_convert_fusion
  372.3 3.1 reshape.363
  375.4 51.0 %all-to-all-done.2 = bf16[16,17,3584]{2,1,0:T(8,128)(2,1)} async-done(((bf16[16,17,3584]{2,1,0:T(8,128)(2,1)}), bf16[16,17,3584]{2,1,0:T(8,128)(2,1)}, u32[]{:S(2)}, u32[]{:S(2)}) %all-to-all-start.2) | async-done | bytes 1949728 | tf_op jit(solution)/shard_map/all_to_all | solution.py:64
  426.4 4.7 all-to-all-start.7
  431.1 2.1 reshape.356
  433.2 2.5 fusion.38
  435.8 4.7 convolution_convert_fusion.2
  440.5 3.1 reshape.357
  443.6 50.8 %all-to-all-done.7 = bf16[16,17,3584]{2,1,0:T(8,128)(2,1)} async-done(((bf16[16,17,3584]{2,1,0:T(8,128)(2,1)}), bf16[16,17,3584]{2,1,0:T(8,128)(2,1)}, u32[]{:S(2)}, u32[]{:S(2)}) %all-to-all-start.7) | async-done | bytes 1949728 | tf_op jit(solution)/shard_map/all_to_all | solution.py:52
  494.5 4.7 all-to-all-start.3
  499.2 0.4 fusion.21
  499.7 0.4 fusion.19
  500.1 2.3 convert_reduce_fusion
  502.4 0.4 fusion.12
  502.8 0.8 maximum_bitcast_fusion.1
  503.6 58.9 %all-to-all-done.3 = bf16[16,17,3584]{2,1,0:T(8,128)(2,1)} async-done(((bf16[16,17,3584]{2,1,0:T(8,128)(2,1)}), bf16[16,17,3584]{2,1,0:T(8,128)(2,1)}, u32[]{:S(2)}, u32[]{:S(2)}) %all-to-all-start.3) | async-done | bytes 1949728 | tf_op jit(solution)/shard_map/all_to_all | solution.py:52
  562.6 2.3 convert_reduce_fusion.2
  564.9 0.4 fusion.13
  565.3 0.8 maximum_bitcast_fusion
  (115 shorter events, 1.5 us)
Async XLA Ops:
  0.6 90.4 %copy-start = (bf16[1,128,3584]{2,1,0:T(8,128)(2,1)S(1)}, bf16[1,128,3584]{2,1,0:T(8,128)(2,1)}, u32[]{:S(2)}) copy-start(bf16[1,128,3584]{2,1,0:T(8,128)(2,1)} %param.19) | copy-start | bytes 2752516
  1.4 231.0 %copy-start.22 = (s32[32]{0:T(128)}, s32[32]{0:T(128)S(1)}, u32[]{:S(2)}) copy-start(s32[32]{0:T(128)S(1)} %get-tuple-element.10) | copy-start | bytes 388
  3.6 220.0 %copy-start.5 = (f32[3584]{0:T(1024)}, f32[3584]{0:T(1024)S(1)}, u32[]{:S(2)}) copy-start(f32[3584]{0:T(1024)S(1)} %reduce) | copy-start | bytes 43012
  6.6 10.6 %copy-start.28 = (s32[2,1,32,1]{2,3,1,0:T(1,128)S(1)}, s32[2,1,32,1]{2,3,1,0:T(1,128)}, u32[]{:S(2)}) copy-start(s32[2,1,32,1]{2,3,1,0:T(1,128)} %param.20) | copy-start | bytes 772
  6.6 11.4 %copy-start.2 = (bf16[1,32,3584]{2,1,0:T(8,128)(2,1)S(1)}, bf16[1,32,3584]{2,1,0:T(8,128)(2,1)}, u32[]{:S(2)}) copy-start(bf16[1,32,3584]{2,1,0:T(8,128)(2,1)} %param.11) | copy-start | bytes 688132
  6.6 74.0 %all-to-all-start.4 = ((bf16[16,17,3584]{2,1,0:T(8,128)(2,1)}), bf16[16,17,3584]{2,1,0:T(8,128)(2,1)}, u32[]{:S(2)}, u32[]{:S(2)}) async-start(bf16[16,17,3584]{2,1,0:T(8,128)(2,1)} %bitcast.185), calls=%async_computation.4 | async-start | bytes 5505024 | tf_op jit(solution)/shard_map/all_to_all | solution.py:64
  17.7 64.6 %copy-start.26 = (s32[32]{0:T(128)}, s32[32]{0:T(128)S(1)}, u32[]{:S(2)}) copy-start(s32[32]{0:T(128)S(1)} %get-tuple-element.13) | copy-start | bytes 388
  18.2 64.2 %copy-start.18 = (pred[2,32]{1,0:T(4,128)(4,1)}, pred[2,32]{1,0:T(4,128)(4,1)S(1)}, u32[]{:S(2)}) copy-start(pred[2,32]{1,0:T(4,128)(4,1)S(1)} %iota_compare_fusion.10) | copy-start | bytes 196
  18.2 64.1 %copy-start.29 = (f32[32]{0:T(128)}, f32[32]{0:T(128)S(1)}, u32[]{:S(2)}) copy-start(f32[32]{0:T(128)S(1)} %add_rsqrt_fusion.3) | copy-start | bytes 388
  18.2 64.1 %copy-start.10 = (pred[17,32]{1,0:T(8,128)(4,1)}, pred[17,32]{1,0:T(8,128)(4,1)S(1)}, u32[]{:S(2)}) copy-start(pred[17,32]{1,0:T(8,128)(4,1)S(1)} %iota_compare_fusion.3) | copy-start | bytes 1636
  82.3 68.1 %all-to-all-start = ((bf16[16,17,3584]{2,1,0:T(8,128)(2,1)}), bf16[16,17,3584]{2,1,0:T(8,128)(2,1)}, u32[]{:S(2)}, u32[]{:S(2)}) async-start(bf16[16,17,3584]{2,1,0:T(8,128)(2,1)} %bitcast.186), calls=%async_computation | async-start | bytes 5505024 | tf_op jit(solution)/shard_map/all_to_all | solution.py:64
  150.5 68.1 %all-to-all-start.5 = ((bf16[16,17,3584]{2,1,0:T(8,128)(2,1)}), bf16[16,17,3584]{2,1,0:T(8,128)(2,1)}, u32[]{:S(2)}, u32[]{:S(2)}) async-start(bf16[16,17,3584]{2,1,0:T(8,128)(2,1)} %reshape.360), calls=%async_computation.5 | async-start | bytes 5505024 | tf_op jit(solution)/shard_map/all_to_all | solution.py:52
  167.0 56.5 %copy-start.1 = (bf16[1,32,3584]{2,1,0:T(8,128)(2,1)S(1)}, bf16[1,32,3584]{2,1,0:T(8,128)(2,1)}, u32[]{:S(2)}) copy-start(bf16[1,32,3584]{2,1,0:T(8,128)(2,1)} %param.12) | copy-start | bytes 688132
  167.0 56.5 %copy-start.35 = (f32[1,3584,2]{1,2,0:T(2,128)S(1)}, f32[1,3584,2]{1,2,0:T(2,128)}, u32[]{:S(2)}) copy-start(f32[1,3584,2]{1,2,0:T(2,128)} %param.16) | copy-start | bytes 86020
  218.6 68.1 %all-to-all-start.1 = ((bf16[16,17,3584]{2,1,0:T(8,128)(2,1)}), bf16[16,17,3584]{2,1,0:T(8,128)(2,1)}, u32[]{:S(2)}, u32[]{:S(2)}) async-start(bf16[16,17,3584]{2,1,0:T(8,128)(2,1)} %reshape.354), calls=%async_computation.1 | async-start | bytes 5505024 | tf_op jit(solution)/shard_map/all_to_all | solution.py:52
  223.9 14.0 %copy-start.16 = (pred[2,32]{1,0:T(4,128)(4,1)}, pred[2,32]{1,0:T(4,128)(4,1)S(1)}, u32[]{:S(2)}) copy-start(pred[2,32]{1,0:T(4,128)(4,1)S(1)} %iota_compare_fusion.4) | copy-start | bytes 196
  224.0 13.8 %copy-start.8 = (bf16[1,32,3584]{2,1,0:T(8,128)(2,1)S(1)}, bf16[1,32,3584]{2,1,0:T(8,128)(2,1)}, u32[]{:S(2)}) copy-start(bf16[1,32,3584]{2,1,0:T(8,128)(2,1)} %param.14) | copy-start | bytes 688132
  224.0 14.0 %copy-start.6 = (f32[3584]{0:T(1024)S(1)}, f32[3584]{0:T(1024)}, u32[]{:S(2)}) copy-start(f32[3584]{0:T(1024)} %copy-done.5) | copy-start | bytes 43012
  226.7 11.0 %collective-permute-start.1 = (bf16[32,3584]{1,0:T(8,128)(2,1)S(1)}, bf16[32,3584]{1,0:T(8,128)(2,1)S(1)}, u32[]{:S(2)}, u32[]{:S(2)}) collective-permute-start(bf16[32,3584]{1,0:T(8,128)(2,1)S(1)} %fusion.10), channel_id=1, source_target_pairs={{16,0},{32,16},{48,32},{64,48},{80,64},{96,80},{112,96},{128,112},... | collective-permute-start | bytes 688136 | tf_op jit(solution)/shard_map/ppermute | solution.py:19
  232.5 55.9 %copy-start.12 = (pred[17,32]{1,0:T(8,128)(4,1)}, pred[17,32]{1,0:T(8,128)(4,1)S(1)}, u32[]{:S(2)}) copy-start(pred[17,32]{1,0:T(8,128)(4,1)S(1)} %iota_compare_fusion) | copy-start | bytes 1636
  238.0 50.4 %copy-start.31 = (f32[32]{0:T(128)}, f32[32]{0:T(128)S(1)}, u32[]{:S(2)}) copy-start(f32[32]{0:T(128)S(1)} %add_rsqrt_fusion) | copy-start | bytes 388
  288.4 4.7 copy-start.24
  288.4 5.0 copy-start.27
  288.4 5.0 copy-start.30
  288.4 68.1 %all-to-all-start.6 = ((bf16[16,17,3584]{2,1,0:T(8,128)(2,1)}), bf16[16,17,3584]{2,1,0:T(8,128)(2,1)}, u32[]{:S(2)}, u32[]{:S(2)}) async-start(bf16[16,17,3584]{2,1,0:T(8,128)(2,1)} %bitcast.184), calls=%async_computation.6 | async-start | bytes 5505024 | tf_op jit(solution)/shard_map/all_to_all | solution.py:64
  293.3 2.9 copy-start.11
  293.3 2.9 copy-start.19
  293.8 14.9 %copy-start.20 = (pred[2,32]{1,0:T(4,128)(4,1)}, pred[2,32]{1,0:T(4,128)(4,1)S(1)}, u32[]{:S(2)}) copy-start(pred[2,32]{1,0:T(4,128)(4,1)S(1)} %iota_compare_fusion.8) | copy-start | bytes 196
  293.8 14.7 %copy-start.9 = (bf16[1,32,3584]{2,1,0:T(8,128)(2,1)S(1)}, bf16[1,32,3584]{2,1,0:T(8,128)(2,1)}, u32[]{:S(2)}) copy-start(bf16[1,32,3584]{2,1,0:T(8,128)(2,1)} %param.13) | copy-start | bytes 688132
  296.6 12.1 %copy-start.3 = (bf16[32,3584]{1,0:T(8,128)(2,1)}, bf16[32,3584]{1,0:T(8,128)(2,1)S(1)}, u32[]{:S(2)}) copy-start(bf16[32,3584]{1,0:T(8,128)(2,1)S(1)} %fusion.8) | copy-start | bytes 688132
  296.6 11.9 %collective-permute-start = (bf16[32,3584]{1,0:T(8,128)(2,1)S(1)}, bf16[32,3584]{1,0:T(8,128)(2,1)S(1)}, u32[]{:S(2)}, u32[]{:S(2)}) collective-permute-start(bf16[32,3584]{1,0:T(8,128)(2,1)S(1)} %fusion.8), channel_id=1, source_target_pairs={{0,16},{16,32},{32,48},{48,64},{64,80},{80,96},{96,112},{112,128},... | collective-permute-start | bytes 688136 | tf_op jit(solution)/shard_map/ppermute | solution.py:19
  300.4 57.9 %copy-start.14 = (pred[17,32]{1,0:T(8,128)(4,1)}, pred[17,32]{1,0:T(8,128)(4,1)S(1)}, u32[]{:S(2)}) copy-start(pred[17,32]{1,0:T(8,128)(4,1)S(1)} %iota_compare_fusion.2) | copy-start | bytes 1636
  308.7 49.6 %copy-start.33 = (f32[32]{0:T(128)}, f32[32]{0:T(128)S(1)}, u32[]{:S(2)}) copy-start(f32[32]{0:T(128)S(1)} %add_rsqrt_fusion.2) | copy-start | bytes 388
  358.3 68.1 %all-to-all-start.2 = ((bf16[16,17,3584]{2,1,0:T(8,128)(2,1)}), bf16[16,17,3584]{2,1,0:T(8,128)(2,1)}, u32[]{:S(2)}, u32[]{:S(2)}) async-start(bf16[16,17,3584]{2,1,0:T(8,128)(2,1)} %bitcast.187), calls=%async_computation.2 | async-start | bytes 5505024 | tf_op jit(solution)/shard_map/all_to_all | solution.py:64
  426.4 68.1 %all-to-all-start.7 = ((bf16[16,17,3584]{2,1,0:T(8,128)(2,1)}), bf16[16,17,3584]{2,1,0:T(8,128)(2,1)}, u32[]{:S(2)}, u32[]{:S(2)}) async-start(bf16[16,17,3584]{2,1,0:T(8,128)(2,1)} %reshape.363), calls=%async_computation.7 | async-start | bytes 5505024 | tf_op jit(solution)/shard_map/all_to_all | solution.py:52
  443.6 55.6 %copy-start.7 = (f32[3584]{0:T(1024)S(1)}, f32[3584]{0:T(1024)}, u32[]{:S(2)}) copy-start(f32[3584]{0:T(1024)} %copy-done.5) | copy-start | bytes 43012
  443.6 55.6 %copy-start.23 = (s32[32]{0:T(128)S(1)}, s32[32]{0:T(128)}, u32[]{:S(2)}) copy-start(s32[32]{0:T(128)} %copy-done.22) | copy-start | bytes 388
  443.6 55.6 %copy-start.32 = (f32[32]{0:T(128)S(1)}, f32[32]{0:T(128)}, u32[]{:S(2)}) copy-start(f32[32]{0:T(128)} %copy-done.31) | copy-start | bytes 388
  443.6 55.6 %copy-start.36 = (f32[1,3584,2]{1,2,0:T(2,128)S(1)}, f32[1,3584,2]{1,2,0:T(2,128)}, u32[]{:S(2)}) copy-start(f32[1,3584,2]{1,2,0:T(2,128)} %param.16) | copy-start | bytes 86020
  443.6 56.0 %copy-start.25 = (s32[32]{0:T(128)S(1)}, s32[32]{0:T(128)}, u32[]{:S(2)}) copy-start(s32[32]{0:T(128)} %get-tuple-element.12) | copy-start | bytes 388
  443.6 56.0 %copy-start.34 = (f32[32]{0:T(128)S(1)}, f32[32]{0:T(128)}, u32[]{:S(2)}) copy-start(f32[32]{0:T(128)} %copy-done.33) | copy-start | bytes 388
  494.5 68.1 %all-to-all-start.3 = ((bf16[16,17,3584]{2,1,0:T(8,128)(2,1)}), bf16[16,17,3584]{2,1,0:T(8,128)(2,1)}, u32[]{:S(2)}, u32[]{:S(2)}) async-start(bf16[16,17,3584]{2,1,0:T(8,128)(2,1)} %reshape.357), calls=%async_computation.3 | async-start | bytes 5505024 | tf_op jit(solution)/shard_map/all_to_all | solution.py:52
  499.7 2.7 copy-start.13
  499.7 2.7 copy-start.17
  503.6 61.2 %copy-start.15 = (pred[17,32]{1,0:T(8,128)(4,1)S(1)}, pred[17,32]{1,0:T(8,128)(4,1)}, u32[]{:S(2)}) copy-start(pred[17,32]{1,0:T(8,128)(4,1)} %copy-done.14) | copy-start | bytes 1636
  503.6 61.3 %copy-start.21 = (pred[2,32]{1,0:T(4,128)(4,1)S(1)}, pred[2,32]{1,0:T(4,128)(4,1)}, u32[]{:S(2)}) copy-start(pred[2,32]{1,0:T(4,128)(4,1)} %copy-done.20) | copy-start | bytes 196
  503.6 61.7 %copy-start.4 = (bf16[32,3584]{1,0:T(8,128)(2,1)S(1)}, bf16[32,3584]{1,0:T(8,128)(2,1)}, u32[]{:S(2)}) copy-start(bf16[32,3584]{1,0:T(8,128)(2,1)} %copy-done.3) | copy-start | bytes 688132
where the time goes:
time: 568 us; the launch traced here: 566 us
  waiting for transfers between devices  435 us (77%)
  starting transfers between devices  52.9 us (9%)
  matrix products  32.9 us (6%)
  local copies, waits for them, and re-layouts  30 us (5%)
  other arithmetic  13.8 us (2%)
    all_to_all x4, waiting for transfers between devices, expert_layer(): lax.all_to_all(outgoing, 'expert', split_axis=0, concat_axis=0, tiled=True)  212 us
    all_to_all x4, waiting for transfers between devices, expert_rows(): lax.all_to_all(part_sum.reshape(received.shape), 'expert', split_axis=0,...  210 us
    all_to_all x4, starting transfers between devices, expert_layer(): lax.all_to_all(outgoing, 'expert', split_axis=0, concat_axis=0, tiled=True)  24.8 us
    dot_general x4, matrix products, expert_rows(): jnp.dot(hidden, down_proj, preferred_element_type=jnp.float32)  18.9 us
    all_to_all x4, starting transfers between devices, expert_rows(): lax.all_to_all(part_sum.reshape(received.shape), 'expert', split_axis=0,...  18.8 us
    ppermute x2, waiting for transfers between devices, passed_along(): return lax.ppermute(block, axis, route)  13.4 us
    reshape x4, local copies, waits for them, and re-layouts, expert_rows(): part_sum.reshape(received.shape)  12.4 us
  transfers between devices with their start and end apart: 10, of which 10 were waited for; matrix products, arithmetic and copies ran while one was open for 11% of the time, Pallas kernels for 0%

commit v1 on v0

v1 whole, which is shorter than its diff:
```python
import jax
import jax.numpy as jnp
from jax import lax
from jax.sharding import PartitionSpec as P

EXP_WIN = 2

epsilon = 1e-06
route_scale = 2.5


def passed_along(block, axis, distance):
    devices = range(lax.axis_size(axis))
    route = [(i - distance, i) for i in devices if i - distance in devices]
    return lax.ppermute(block, axis, route)


def normalize(tokens, gains):
    widened = tokens.astype(jnp.float32)
    inverse = lax.rsqrt(jnp.mean(widened * widened, axis=-1, keepdims=True) + epsilon)
    return (widened * inverse * gains[None, :]).astype(jnp.bfloat16)


def gate_weight(normed, router, route):
    scores = jnp.dot(normed.astype(jnp.float32), router, precision=lax.Precision.HIGHEST)
    onehot = (route == jnp.arange(EXP_WIN, dtype=jnp.int32)[None, :]).astype(jnp.float32)
    return route_scale * jax.nn.sigmoid(jnp.sum(scores * onehot, axis=1, keepdims=True))


def layer(tokens, route, all_routes, gains, router, both, down_proj, mine):
    normed = normalize(tokens, gains)
    everyone = lax.all_gather(normed, "expert", axis=0, tiled=True)
    weight = gate_weight(normed, router, route)
    acts = jnp.dot(everyone, both, preferred_element_type=jnp.float32)
    units = acts.shape[1] // 2
    hidden = jax.nn.silu(acts[:, :units]) * acts[:, units:]
    hidden = jnp.where(all_routes == mine, hidden, 0.0).astype(jnp.bfloat16)
    part = jnp.dot(hidden, down_proj, preferred_element_type=jnp.float32).astype(jnp.bfloat16)
    expert_out = lax.psum_scatter(part, "expert", scatter_dimension=0, tiled=True)
    return (tokens.astype(jnp.float32) + weight * expert_out.astype(jnp.float32)).astype(
        jnp.bfloat16
    )


def shards(
    first_state,
    second_state,
    first_enter,
    second_enter,
    norm_gain,
    router,
    gate_proj,
    up_proj,
    down_proj,
    first_routes,
    second_routes,
):
    gains = norm_gain[0]
    router_cols = router[0]
    both = jnp.concatenate([gate_proj[0], up_proj[0]], axis=1)
    down_local = down_proj[0]
    position = lax.axis_index("pipe")
    final_section = lax.axis_size("pipe") - 1
    mine = lax.axis_index("expert") // (lax.axis_size("expert") // EXP_WIN)
    routes = jnp.stack([first_routes[:, 0], second_routes[:, 0]])
    all_routes = lax.all_gather(routes, "expert", axis=2, tiled=True)
    now = [first_state[0], second_state[0]]
    done = [[], []]
    for step_index in range(first_routes.shape[0]):
        if step_index > 0:
            first_moved = passed_along(done[0][-1], "pipe", 1)
            second_moved = passed_along(done[1][-1], "pipe", -1)
            now = [
                jnp.where(position == 0, first_enter[step_index - 1], first_moved),
                jnp.where(position == final_section, second_enter[step_index - 1], second_moved),
            ]
        for which in range(2):
            done[which].append(
                layer(
                    now[which],
                    routes[which, step_index],
                    all_routes[which, step_index],
                    gains,
                    router_cols,
                    both,
                    down_local,
                    mine,
                )
            )
    return (jnp.stack(done[0])[:, None], jnp.stack(done[1])[:, None])


def solution(mesh):
    return jax.shard_map(
        shards,
        mesh=mesh,
        in_specs=(
            P("pipe", "expert", None),
            P("pipe", "expert", None),
            P(None, "expert", None),
            P(None, "expert", None),
            P("pipe", None),
            P("pipe", None, None),
            P("pipe", None, "expert"),
            P("pipe", None, "expert"),
            P("pipe", "expert", None),
            P(None, "pipe", "expert", None),
            P(None, "pipe", "expert", None),
        ),
        out_specs=(P(None, "pipe", "expert", None), P(None, "pipe", "expert", None)),
        check_vma=False,
    )
```

time: 568 us -> 490 us (0.86); the launches traced: 566 us -> 481 us
  waiting for transfers between devices: 435 us -> 353 us
  starting transfers between devices: 52.9 us -> 8.56 us
  other arithmetic: 13.8 us -> 51.5 us
  local copies, waits for them, and re-layouts: 30 us -> 1.19 us
  blocking collectives: 0 us -> 25.1 us
  between operations: 1.37 us -> 14.9 us
  matrix products: 32.9 us -> 27.1 us
    all_to_all x8 -> x0, waiting for transfers between devices: 422 us -> none  [the longest x4 212 us: expert_layer(): lax.all_to_all(outgoing, 'expert', split_axis=0, concat_axis=0, tiled=True)]
    reduce_scatter x0 -> x4, waiting for transfers between devices: none -> 243 us  [layer(): lax.psum_scatter(part, 'expert', scatter_dimension=0, tiled=True)]
    all_gather x0 -> x4, waiting for transfers between devices: none -> 105 us  [layer(): everyone = lax.all_gather(normed, 'expert', axis=0, tiled=True)]
    all_to_all x8 -> x0, starting transfers between devices: 43.6 us -> none  [the longest x4 24.8 us: expert_layer(): lax.all_to_all(outgoing, 'expert', split_axis=0, concat_axis=0, tiled=True)]
    eq x8 -> x1, other arithmetic: 0.06 us -> 38.5 us  [layer(): hidden = jnp.where(all_routes == mine, hidden, 0.0).astype(jnp.bfloat16)]
    all_gather x0 -> x1, blocking collectives: none -> 25.1 us  [shards(): all_routes = lax.all_gather(routes, 'expert', axis=2, tiled=True)]
    reshape x8 -> x0, local copies, waits for them, and re-layouts: 20.9 us -> none  [the longest x4 12.4 us: expert_rows(): part_sum.reshape(received.shape)]
    ppermute x2, waiting for transfers between devices: 13.4 us -> 3.29 us  [passed_along(): return lax.ppermute(block, axis, route)]
  transfers between devices with their start and end apart: 10 -> 10, of which waited for: 10 -> 8; matrix products, arithmetic and copies ran while one was open for 11% -> 15% of each run, Pallas kernels for 0% -> 0%
where the time goes in v1:
time: 490 us; the launch traced here: 481 us
  waiting for transfers between devices  353 us (72%)
  other arithmetic  51.5 us (11%)
  matrix products  27.1 us (6%)
  blocking collectives  25.1 us (5%)
  between operations  14.9 us (3%)
  starting transfers between devices  8.56 us (2%)
    reduce_scatter x4, waiting for transfers between devices, layer(): lax.psum_scatter(part, 'expert', scatter_dimension=0, tiled=True)  243 us
    all_gather x4, waiting for transfers between devices, layer(): everyone = lax.all_gather(normed, 'expert', axis=0, tiled=True)  105 us
    eq x1, other arithmetic, layer(): hidden = jnp.where(all_routes == mine, hidden, 0.0).astype(jnp.bfloat16)  38.5 us
    all_gather x1, blocking collectives, shards(): all_routes = lax.all_gather(routes, 'expert', axis=2, tiled=True)  25.1 us
    dot_general x4, matrix products, layer(): acts = jnp.dot(everyone, both, preferred_element_type=jnp.float32)  13.7 us
    dot_general x4, matrix products, layer(): jnp.dot(hidden, down_proj, preferred_element_type=jnp.float32)  12 us
  transfers between devices with their start and end apart: 10, of which 8 were waited for; matrix products, arithmetic and copies ran while one was open for 15% of the time, Pallas kernels for 0%

profile of v1, /device:TPU:6, one launch (start us, length us, event | category | flops | bytes accessed | tf_op | source)
XLA Modules:
  0.0 480.8 jit_solution(17624862318026065049)
XLA Ops:
  7.2 0.0 copy-start
  7.2 0.0 all-gather.5.cloned.1.call-start
  7.2 1.2 fusion.14
  8.4 1.1 fusion.20
  9.5 0.8 reduce
  10.3 2.0 fusion.22
  12.2 0.0 all-gather.5.cloned.1.call-update
  12.3 0.0 all-gather.9.cloned.1.call-start
  12.3 0.7 all-gather.9.cloned.1.call-update
  13.0 0.0 reduce-scatter.5.cloned.1.call-start
  13.1 0.7 pad_add_fusion
  13.8 0.1 copy.18
  13.9 25.1 %all_gather.15 = s32[2,2,512,1]{1,0,3,2:T(2,128)S(1)} all-gather(s32[2,2,32,1]{1,0,3,2:T(2,128)S(1)} %copy.18), channel_id=1, replica_groups=mesh['pipe'=32,'expert'=16] {'expert'}, dimensions={2}, use_global_device_ids=true | all-gather | bytes 8704 | tf_op jit(solution)/shard_map/all_gather | solution.py:66
  39.0 38.5 %compare_reduce_fusion = (pred[512]{0:T(512)(128)(4,1)S(1)}, pred[512]{0:T(512)(128)(4,1)S(1)}, pred[512]{0:T(512)(128)(4,1)S(1)}, pred[512]{0:T(512)(128)(4,1)S(1)}) fusion(s32[2,2,512,1]{1,0,3,2:T(2,128)S(1)} %all_gather.15, s32[]{:T(128)S(6)} %select_n.32), kind=kLoop, calls=%fused_computation.13 | loop fusion | flops 2048 | bytes 10244 | tf_op jit(solution)/shard_map/eq | solution.py:37
  77.5 0.0 all-gather.5.cloned.1.call-done
  77.5 3.7 fusion.83
  81.2 0.0 copy-start.9
  81.2 0.0 copy-start.10
  81.2 3.0 convolution_convert_fusion.3
  84.2 0.0 reduce-scatter.5.cloned.1.call-update
  84.2 0.0 reduce-scatter.9.cloned.1.call-start
  84.3 23.4 %all-gather.9.cloned.1.call-done = bf16[512,3584]{1,0:T(8,128)(2,1)} async-done(((bf16[32,3584]{1,0:T(8,128)(2,1)}), bf16[512,3584]{1,0:T(8,128)(2,1)}) %all-gather.9.cloned.1.call-update) | async-done | bytes 3670032 | tf_op jit(solution)/shard_map/all_gather | solution.py:32
  107.7 3.2 fusion.81
  110.9 0.0 copy-start.7
  110.9 0.0 copy-start.11
  111.0 3.0 convolution_convert_fusion.1
  114.0 0.0 reduce-scatter.9.cloned.1.call-update
  114.0 0.0 all-gather.11.cloned.1.call-start
  114.1 0.4 fusion
  114.5 0.2 copy-done.8
  114.7 0.3 copy-done.2
  114.9 0.4 fusion.2
  115.3 58.7 %reduce-scatter.5.cloned.1.call-done = bf16[32,3584]{1,0:T(8,128)(2,1)} async-done(((bf16[512,3584]{1,0:T(8,128)(2,1)}), bf16[32,3584]{1,0:T(8,128)(2,1)}) %reduce-scatter.5.cloned.1.call-update) | async-done | bytes 229392 | tf_op jit(solution)/shard_map/reduce_scatter | solution.py:39
  174.0 1.1 fusion.17
  175.1 3.4 collective-permute-start
  178.5 61.4 %reduce-scatter.9.cloned.1.call-done = bf16[32,3584]{1,0:T(8,128)(2,1)} async-done(((bf16[512,3584]{1,0:T(8,128)(2,1)}), bf16[32,3584]{1,0:T(8,128)(2,1)}) %reduce-scatter.9.cloned.1.call-update) | async-done | bytes 229392 | tf_op jit(solution)/shard_map/reduce_scatter | solution.py:39
  239.9 1.1 fusion.23
  241.0 4.8 %collective-permute-start.1 = (bf16[32,3584]{1,0:T(8,128)(2,1)S(1)}, bf16[32,3584]{1,0:T(8,128)(2,1)S(1)}, u32[]{:S(2)}, u32[]{:S(2)}) collective-permute-start(bf16[32,3584]{1,0:T(8,128)(2,1)S(1)} %fusion.23), channel_id=1, source_target_pairs={{16,0},{32,16},{48,32},{64,48},{80,64},{96,80},{112,96},{128,112},... | collective-permute-start | bytes 688136 | tf_op jit(solution)/shard_map/ppermute | solution.py:15
  245.9 0.2 fusion.26
  246.1 3.3 collective-permute-done.1
  249.4 0.2 fusion.30
  249.6 0.9 fusion.32
  250.5 0.0 all-gather.11.cloned.1.call-update
  250.6 0.0 all-gather.7.cloned.1.call-start
  250.6 0.5 all-gather.7.cloned.1.call-update
  251.1 0.0 reduce-scatter.11.cloned.1.call-start
  251.2 42.6 %all-gather.11.cloned.1.call-done = bf16[512,3584]{1,0:T(8,128)(2,1)} async-done(((bf16[32,3584]{1,0:T(8,128)(2,1)}), bf16[512,3584]{1,0:T(8,128)(2,1)}) %all-gather.11.cloned.1.call-update) | async-done | bytes 3670032 | tf_op jit(solution)/shard_map/all_gather | solution.py:32
  293.8 3.4 fusion.80
  297.2 3.0 convolution_convert_fusion
  300.2 0.0 reduce-scatter.11.cloned.1.call-update
  300.2 0.0 reduce-scatter.7.cloned.1.call-start
  300.3 39.2 %all-gather.7.cloned.1.call-done = bf16[512,3584]{1,0:T(8,128)(2,1)} async-done(((bf16[32,3584]{1,0:T(8,128)(2,1)}), bf16[512,3584]{1,0:T(8,128)(2,1)}) %all-gather.7.cloned.1.call-update) | async-done | bytes 3670032 | tf_op jit(solution)/shard_map/all_gather | solution.py:32
  339.5 3.4 fusion.82
  342.9 3.0 convolution_convert_fusion.2
  346.0 0.0 reduce-scatter.7.cloned.1.call-update
  346.0 0.3 fusion.3
  346.3 0.6 copy-done.3
  346.9 0.3 fusion.1
  347.2 58.6 %reduce-scatter.11.cloned.1.call-done = bf16[32,3584]{1,0:T(8,128)(2,1)} async-done(((bf16[512,3584]{1,0:T(8,128)(2,1)}), bf16[32,3584]{1,0:T(8,128)(2,1)}) %reduce-scatter.11.cloned.1.call-update) | async-done | bytes 229392 | tf_op jit(solution)/shard_map/reduce_scatter | solution.py:39
  405.8 1.1 fusion.42
  406.9 0.8 maximum_bitcast_fusion.1
  407.7 64.0 %reduce-scatter.7.cloned.1.call-done = bf16[32,3584]{1,0:T(8,128)(2,1)} async-done(((bf16[512,3584]{1,0:T(8,128)(2,1)}), bf16[32,3584]{1,0:T(8,128)(2,1)}) %reduce-scatter.7.cloned.1.call-update) | async-done | bytes 229392 | tf_op jit(solution)/shard_map/reduce_scatter | solution.py:39
  471.7 1.1 fusion.43
  472.7 0.8 maximum_bitcast_fusion
  (26 shorter events, 0.1 us)
Async XLA Ops:
  7.2 74.0 %copy-start = (bf16[1,128,3584]{2,1,0:T(8,128)(2,1)S(1)}, bf16[1,128,3584]{2,1,0:T(8,128)(2,1)}, u32[]{:S(2)}) copy-start(bf16[1,128,3584]{2,1,0:T(8,128)(2,1)} %param.19) | copy-start | bytes 2752516
  7.2 70.3 %all-gather.5.cloned.1.call-start = ((), (), s32[]{:S(2)}) async-start(), calls=%async_computation.4 | async-start | bytes 3899392 | tf_op jit(solution)/shard_map/all_gather | solution.py:32
  12.3 95.4 %all-gather.9.cloned.1.call-start = ((), (), s32[]{:S(2)}) async-start(), calls=%async_computation.8 | async-start | bytes 3899392 | tf_op jit(solution)/shard_map/all_gather | solution.py:32
  13.0 161.0 %reduce-scatter.5.cloned.1.call-start = ((), (), s32[]{:S(2)}) async-start(), calls=%async_computation.5 | async-start | bytes 3899392 | tf_op jit(solution)/shard_map/reduce_scatter | solution.py:39
  81.2 26.5 %copy-start.9 = (bf16[1,3584,128]{2,1,0:T(8,128)(2,1)S(1)}, bf16[1,3584,128]{2,1,0:T(8,128)(2,1)}, u32[]{:S(2)}) copy-start(bf16[1,3584,128]{2,1,0:T(8,128)(2,1)} %param.18) | copy-start | bytes 2752516
  81.2 26.5 %copy-start.10 = (bf16[1,3584,128]{2,1,0:T(8,128)(2,1)S(1)}, bf16[1,3584,128]{2,1,0:T(8,128)(2,1)}, u32[]{:S(2)}) copy-start(bf16[1,3584,128]{2,1,0:T(8,128)(2,1)} %param.17) | copy-start | bytes 2752516
  84.2 155.7 %reduce-scatter.9.cloned.1.call-start = ((), (), s32[]{:S(2)}) async-start(), calls=%async_computation.9 | async-start | bytes 3899392 | tf_op jit(solution)/shard_map/reduce_scatter | solution.py:39
  110.9 3.1 copy-start.7
  110.9 3.2 copy-start.1
  110.9 3.2 copy-start.11
  114.0 0.7 copy-start.8
  114.0 1.0 copy-start.2
  114.0 131.9 %copy-start.5 = (bf16[1,32,3584]{2,1,0:T(8,128)(2,1)S(1)}, bf16[1,32,3584]{2,1,0:T(8,128)(2,1)}, u32[]{:S(2)}) copy-start(bf16[1,32,3584]{2,1,0:T(8,128)(2,1)} %param.13) | copy-start | bytes 688132
  114.0 135.4 %copy-start.6 = (bf16[1,32,3584]{2,1,0:T(8,128)(2,1)S(1)}, bf16[1,32,3584]{2,1,0:T(8,128)(2,1)}, u32[]{:S(2)}) copy-start(bf16[1,32,3584]{2,1,0:T(8,128)(2,1)} %param.14) | copy-start | bytes 688132
  114.0 179.8 %all-gather.11.cloned.1.call-start = ((), (), s32[]{:S(2)}) async-start(), calls=%async_computation.10 | async-start | bytes 3899392 | tf_op jit(solution)/shard_map/all_gather | solution.py:32
  175.1 70.7 %collective-permute-start = (bf16[32,3584]{1,0:T(8,128)(2,1)S(1)}, bf16[32,3584]{1,0:T(8,128)(2,1)S(1)}, u32[]{:S(2)}, u32[]{:S(2)}) collective-permute-start(bf16[32,3584]{1,0:T(8,128)(2,1)S(1)} %fusion.17), channel_id=1, source_target_pairs={{0,16},{16,32},{32,48},{48,64},{64,80},{80,96},{96,112},{112,128},... | collective-permute-start | bytes 688136 | tf_op jit(solution)/shard_map/ppermute | solution.py:15
  241.0 8.4 %collective-permute-start.1 = (bf16[32,3584]{1,0:T(8,128)(2,1)S(1)}, bf16[32,3584]{1,0:T(8,128)(2,1)S(1)}, u32[]{:S(2)}, u32[]{:S(2)}) collective-permute-start(bf16[32,3584]{1,0:T(8,128)(2,1)S(1)} %fusion.23), channel_id=1, source_target_pairs={{16,0},{32,16},{48,32},{64,48},{80,64},{96,80},{112,96},{128,112},... | collective-permute-start | bytes 688136 | tf_op jit(solution)/shard_map/ppermute | solution.py:15
  250.6 88.9 %all-gather.7.cloned.1.call-start = ((), (), s32[]{:S(2)}) async-start(), calls=%async_computation.6 | async-start | bytes 3899392 | tf_op jit(solution)/shard_map/all_gather | solution.py:32
  251.1 154.7 %reduce-scatter.11.cloned.1.call-start = ((), (), s32[]{:S(2)}) async-start(), calls=%async_computation.11 | async-start | bytes 3899392 | tf_op jit(solution)/shard_map/reduce_scatter | solution.py:39
  300.2 171.4 %reduce-scatter.7.cloned.1.call-start = ((), (), s32[]{:S(2)}) async-start(), calls=%async_computation.7 | async-start | bytes 3899392 | tf_op jit(solution)/shard_map/reduce_scatter | solution.py:39
  342.9 3.1 copy-start.4
  345.9 0.9 copy-start.3
Sparse Core Ops, SparseCore 0:
  12.4 49.9 all-gather.4
  65.1 42.5 all-gather.8
  110.6 63.4 reduce-scatter.4
  176.8 63.1 reduce-scatter.8
  250.7 43.0 all-gather.10
  296.3 43.0 all-gather.6
  342.3 63.4 reduce-scatter.10
  408.7 62.9 reduce-scatter.6

commit v2 on v1

v2 whole, which is shorter than its diff:
```python
import functools

import jax
import jax.numpy as jnp
from jax import lax
from jax.experimental import pallas as pl
from jax.experimental.pallas import tpu as pltpu
from jax.sharding import PartitionSpec as P

EXP_WIN = 2
MESH = pl.DeviceIdType.MESH

epsilon = 1e-06
route_scale = 2.5

BELOW = (1, 6, 4, 2, 0)
ABOVE = (1, 7, 5, 3, 0)
SLOTS = 8
CHUNKS = 4
GATHER_UP = ((0, 0), (0, 1), (1, 0), (1, 1), (2, 0), (2, 1), (3, 0))
GATHER_DOWN = ((0, 1), (0, 0), (1, 1), (1, 0), (2, 1), (2, 0), (3, 1))
REDUCE_UP = ((4, 0), (3, 1), (3, 0), (2, 1), (2, 0), (1, 1), (1, 0))
REDUCE_DOWN = ((4, 1), (3, 0), (3, 1), (2, 0), (2, 1), (1, 0), (1, 1))
UNITS = 7
LANES = 128


def relay_kernel(
    chips,
    sections,
    first_state,
    second_state,
    first_enter,
    second_enter,
    gains,
    router,
    gate_hbm,
    up_hbm,
    down_hbm,
    first_routes,
    second_routes,
    first_out,
    second_out,
    held,
    part,
    sib_part,
    from_below,
    from_above,
    arrived,
    current,
    weight,
    both,
    down,
    named,
    gu_s,
    gu_r,
    gd_s,
    gd_r,
    gs_s,
    gs_r,
    ru_s,
    ru_r,
    rd_s,
    rd_r,
    rs_s,
    rs_r,
    pipe_s,
    pipe_r,
    nu_s,
    nu_r,
    nd_s,
    nd_r,
    ns_s,
    ns_r,
    load_sem,
):
    rows, width = current.shape[1:]
    half_rows = rows // 2
    units = down.shape[0]
    e = lax.axis_index("expert")
    p = lax.axis_index("pipe")
    z, c = e // 2, e % 2
    mine = (z // (chips // EXP_WIN)).astype(jnp.float32)
    above = {"expert": ((z + 1) % chips) * 2 + c}
    below = {"expert": ((z + chips - 1) % chips) * 2 + c}
    sibling = {"expert": z * 2 + (1 - c)}
    onward = {"pipe": (p + 1) % sections}
    backward = {"pipe": (p + sections - 1) % sections}
    routes = (first_routes, second_routes)
    states = (first_state, second_state)
    enters = (first_enter, second_enter)
    outs = (first_out, second_out)

    def remote(src, dst, send, recv, device):
        return pltpu.make_async_remote_copy(
            src_ref=src,
            dst_ref=dst,
            send_sem=send,
            recv_sem=recv,
            device_id=device,
            device_id_type=MESH,
        )

    def half(index):
        return pl.ds(index * half_rows, half_rows)

    def gather_copy(t, s, j, up):
        d, h = (GATHER_UP if up else GATHER_DOWN)[j]
        slots = BELOW if up else ABOVE
        return remote(
            held.at[t, s, slots[d], c, half(h)],
            held.at[t, s, slots[d + 1], c, half(h)],
            (gu_s if up else gd_s).at[t, s, j],
            (gu_r if up else gd_r).at[t, s, j],
            above if up else below,
        )

    def gather_sibling(t, s, slot, core):
        ref = held.at[t, s, slot, core]
        return remote(ref, ref, gs_s.at[t, s, slot], gs_r.at[t, s, slot], sibling)

    def names_copy(d, up):
        slots = BELOW if up else ABOVE
        return remote(
            named.at[slots[d], c],
            named.at[slots[d + 1], c],
            (nu_s if up else nd_s).at[d],
            (nu_r if up else nd_r).at[d],
            above if up else below,
        )

    def names_sibling(slot, core):
        ref = named.at[slot, core]
        return remote(ref, ref, ns_s.at[slot], ns_r.at[slot], sibling)

    def start_gather(t, s, first=False):
        if first:
            names_copy(0, True).start()
            names_copy(0, False).start()
        for j in range(2):
            gather_copy(t, s, j, True).start()
            gather_copy(t, s, j, False).start()
        if first:
            names_sibling(1, c).start()
        gather_sibling(t, s, 1, c).start()

    def gather_step(t, s, j):
        for up in (True, False):
            gather_copy(t, s, j, up).wait_recv()
            if j + 2 < UNITS:
                gather_copy(t, s, j + 2, up).start()
        if j % 2 == 1:
            d = j // 2
            for slots in (BELOW, ABOVE):
                gather_sibling(t, s, slots[d + 1], c).start()
        if j == UNITS - 1:
            gather_sibling(t, s, 0, c).start()
        if s == 0 and j % 2 == 1:

            @pl.when(t == 0)
            def _():
                d = j // 2
                for up, slots in ((True, BELOW), (False, ABOVE)):
                    names_copy(d, up).wait_recv()
                    if d + 1 < (4 if up else 3):
                        names_copy(d + 1, up).start()
                    names_sibling(slots[d + 1], c).start()

        if s == 0 and j == UNITS - 1:

            @pl.when(t == 0)
            def _():
                names_copy(3, True).wait_recv()
                names_sibling(0, c).start()

    def finish_gather(t, s):
        for j in range(UNITS):
            gather_copy(t, s, j, True).wait_send()
            gather_copy(t, s, j, False).wait_send()
        for slot in range(SLOTS):
            gather_sibling(t, s, slot, c).wait_send()

    def part_sibling(t, s, slot):
        return remote(
            part.at[t, s, slot, 1 - c],
            sib_part.at[t, s, slot],
            rs_s.at[t, s, slot],
            rs_r.at[t, s, slot],
            sibling,
        )

    def compute(t, s, q):
        pair = pl.ds(2 * q, 2)
        for slot in (2 * q, 2 * q + 1):
            gather_sibling(t, s, slot, 1 - c).wait_recv()
        if s == 0:

            @pl.when(t == 0)
            def _():
                for slot in (2 * q, 2 * q + 1):
                    names_sibling(slot, 1 - c).wait_recv()

        count = 4 * rows
        tokens = held[t, s, pair].reshape(count, width)
        acts = jnp.dot(tokens, both[...], preferred_element_type=jnp.float32)
        gate_act, up_act = acts[:, :units], acts[:, units:]
        lane = lax.broadcasted_iota(jnp.int32, (count, LANES), 1)
        names = named[pair].reshape(count, LANES).astype(jnp.float32)
        name = jnp.sum(jnp.where(lane == 2 * t + s, names, 0.0), axis=1, keepdims=True)
        hidden = gate_act * jax.nn.sigmoid(gate_act) * up_act
        hidden = jnp.where(name == mine, hidden, 0.0).astype(jnp.bfloat16)
        step = 512
        for start in range(0, width, step):
            cols = pl.ds(start, step)
            product = jnp.dot(hidden, down[:, cols], preferred_element_type=jnp.float32)
            part[t, s, pair, :, :, cols] = product.astype(jnp.bfloat16).reshape(2, 2, rows, step)
        for slot in (2 * q, 2 * q + 1):
            part_sibling(t, s, slot).start()

    def reduce_copy(t, s, j, up):
        d, h = (REDUCE_UP if up else REDUCE_DOWN)[j]
        slot = (ABOVE if up else BELOW)[d]
        return remote(
            part.at[t, s, slot, c, half(h)],
            (from_below if up else from_above).at[t, s, d - 1, half(h)],
            (ru_s if up else rd_s).at[t, s, j],
            (ru_r if up else rd_r).at[t, s, j],
            above if up else below,
        )

    def reduce_send(t, s, j, up):
        d, h = (REDUCE_UP if up else REDUCE_DOWN)[j]
        slot = (ABOVE if up else BELOW)[d]
        total = part[t, s, slot, c, half(h)].astype(jnp.float32)
        total = total + sib_part[t, s, slot, half(h)].astype(jnp.float32)
        if j >= 2:
            came = from_below if up else from_above
            total = total + came[t, s, d, half(h)].astype(jnp.float32)
        part[t, s, slot, c, half(h)] = total.astype(jnp.bfloat16)
        reduce_copy(t, s, j, up).start()

    def start_reduce(t, s):
        part_sibling(t, s, 0).wait_recv()
        for up in (True, False):
            reduce_send(t, s, 0, up)
        for up in (True, False):
            part_sibling(t, s, (ABOVE if up else BELOW)[3]).wait_recv()
            reduce_send(t, s, 1, up)

    def reduce_step(t, s, j):
        if j in (1, 3):
            for slots in (ABOVE, BELOW):
                part_sibling(t, s, slots[2 if j == 1 else 1]).wait_recv()
        for up in (True, False):
            reduce_copy(t, s, j, up).wait_recv()
            if j + 2 < UNITS:
                reduce_send(t, s, j + 2, up)

    def finish_reduce(t, s):
        for j in range(UNITS):
            reduce_copy(t, s, j, True).wait_send()
            reduce_copy(t, s, j, False).wait_send()
        for slot in range(SLOTS):
            part_sibling(t, s, slot).wait_send()

    def normalize(t, s):
        route = routes[s][t]
        for h in range(2):
            rows_of = half(h)
            widened = current[s, rows_of].astype(jnp.float32)
            mean = jnp.mean(widened * widened, axis=-1, keepdims=True)
            normed = widened * lax.rsqrt(mean + epsilon) * gains[...]
            normed = normed.astype(jnp.bfloat16)
            held[t, s, 1, c, rows_of] = normed
            chosen = route[h * half_rows : (h + 1) * half_rows]
            column = jnp.where(chosen == 0, router[0:1], router[1:2])
            score = jnp.sum(normed.astype(jnp.float32) * column, axis=1, keepdims=True)
            weight[s, rows_of] = jnp.broadcast_to(
                route_scale * jax.nn.sigmoid(score), (half_rows, LANES)
            )

    def pipe_copy(s):
        return remote(
            outs[s].at[0],
            arrived.at[s],
            pipe_s.at[s],
            pipe_r.at[s],
            onward if s == 0 else backward,
        )

    def receive(s):
        pipe_copy(s).wait_recv()
        current[s] = arrived[s]

        @pl.when(p == (0 if s == 0 else sections - 1))
        def _():
            current[s] = enters[s][0]

    def finalize(t, s):
        part_sibling(t, s, 1).wait_recv()
        for h in range(2):
            rows_of = half(h)
            total = part[t, s, 1, c, rows_of].astype(jnp.float32)
            total = total + sib_part[t, s, 1, rows_of].astype(jnp.float32)
            total = total + from_below[t, s, 0, rows_of].astype(jnp.float32)
            total = total + from_above[t, s, 0, rows_of].astype(jnp.float32)
            widened = current[s, rows_of].astype(jnp.float32)
            result = widened + weight[s, rows_of, 0:1] * total
            outs[s][t, rows_of] = result.astype(jnp.bfloat16)

        @pl.when(t == 0)
        def _():
            pipe_copy(s).start()

    barrier = pltpu.get_barrier_semaphore()
    partners = (above, below, sibling, onward, backward)
    for partner in partners:
        pl.semaphore_signal(barrier, inc=1, device_id=partner, device_id_type=MESH)
    loads = (
        pltpu.make_async_copy(gate_hbm, both.at[:, pl.ds(0, units)], load_sem.at[0]),
        pltpu.make_async_copy(up_hbm, both.at[:, pl.ds(units, units)], load_sem.at[1]),
        pltpu.make_async_copy(down_hbm, down, load_sem.at[2]),
    )
    for load in loads:
        load.start()
    lane = lax.broadcasted_iota(jnp.int32, (rows, LANES), 1)
    own = jnp.zeros((rows, LANES), jnp.float32)
    for step in range(2):
        for s in range(2):
            own = jnp.where(lane == 2 * step + s, routes[s][step].astype(jnp.float32), own)
    named[1, c] = own.astype(jnp.bfloat16)
    current[0] = states[0][0]
    normalize(0, 0)
    pl.semaphore_wait(barrier, len(partners))
    start_gather(0, 0, first=True)
    current[1] = states[1][0]
    normalize(0, 1)
    for load in loads:
        load.wait()

    def one_step(t, carry):
        for j in range(UNITS):
            gather_step(t, 0, j)
            if j == 3:

                @pl.when(t > 0)
                def _():
                    receive(1)
                    normalize(t, 1)

                start_gather(t, 1)
        for j in range(UNITS):
            gather_step(t, 1, j)
            if j < CHUNKS:
                compute(t, 0, j)
            if j == 5:
                start_reduce(t, 0)
        for j in range(UNITS):
            reduce_step(t, 0, j)
            if j < CHUNKS:
                compute(t, 1, j)
            if j == 5:
                start_reduce(t, 1)
        finalize(t, 0)
        for j in range(UNITS):
            reduce_step(t, 1, j)
            if j == 3:

                @pl.when(t == 0)
                def _():
                    receive(0)
                    normalize(1, 0)
                    start_gather(1, 0)

        finalize(t, 1)
        for s in range(2):
            finish_gather(t, s)
            finish_reduce(t, s)
        return carry

    lax.fori_loop(0, 2, one_step, 0)
    for s in range(2):
        pipe_copy(s).wait_send()
    for d in range(4):
        names_copy(d, True).wait_send()
    for d in range(3):
        names_copy(d, False).wait_send()
    for slot in range(SLOTS):
        names_sibling(slot, c).wait_send()


def shards(
    first_state,
    second_state,
    first_enter,
    second_enter,
    norm_gain,
    router,
    gate_proj,
    up_proj,
    down_proj,
    first_routes,
    second_routes,
):
    chips = lax.axis_size("expert") // 2
    sections = lax.axis_size("pipe")
    rows, width = first_state.shape[1:]
    units = gate_proj.shape[2]
    steps = first_routes.shape[0]
    vmem = pl.BlockSpec(memory_space=pltpu.VMEM)
    hbm = pl.BlockSpec(memory_space=pl.ANY)
    bf16 = jnp.bfloat16
    dma = pltpu.SemaphoreType.DMA
    out = jax.ShapeDtypeStruct((steps, rows, width), bf16)
    outs = pl.pallas_call(
        functools.partial(relay_kernel, chips, sections),
        out_shape=(out, out),
        in_specs=[vmem] * 6 + [hbm] * 3 + [vmem] * 2,
        out_specs=(vmem, vmem),
        scratch_shapes=[
            pltpu.VMEM((steps, 2, SLOTS, 2, rows, width), bf16),
            pltpu.VMEM((steps, 2, SLOTS, 2, rows, width), bf16),
            pltpu.VMEM((steps, 2, SLOTS, rows, width), bf16),
            pltpu.VMEM((steps, 2, 4, rows, width), bf16),
            pltpu.VMEM((steps, 2, 4, rows, width), bf16),
            pltpu.VMEM((2, rows, width), bf16),
            pltpu.VMEM((2, rows, width), bf16),
            pltpu.VMEM((2, rows, LANES), jnp.float32),
            pltpu.VMEM((width, 2 * units), bf16),
            pltpu.VMEM((units, width), bf16),
            pltpu.VMEM((SLOTS, 2, rows, LANES), bf16),
        ]
        + [dma((steps, 2, UNITS))] * 4
        + [dma((steps, 2, SLOTS))] * 2
        + [dma((steps, 2, UNITS))] * 4
        + [dma((steps, 2, SLOTS))] * 2
        + [dma((2,))] * 2
        + [dma((4,))] * 4
        + [dma((SLOTS,))] * 2
        + [dma((3,))],
        compiler_params=pltpu.CompilerParams(
            collective_id=0, has_side_effects=True, vmem_limit_bytes=60 << 20
        ),
        name="relay_window",
    )(
        first_state,
        second_state,
        first_enter,
        second_enter,
        norm_gain,
        router[0].T,
        gate_proj[0],
        up_proj[0],
        down_proj[0],
        first_routes[:, 0],
        second_routes[:, 0],
    )
    return (outs[0][:, None], outs[1][:, None])


def solution(mesh):
    return jax.shard_map(
        shards,
        mesh=mesh,
        in_specs=(
            P("pipe", "expert", None),
            P("pipe", "expert", None),
            P(None, "expert", None),
            P(None, "expert", None),
            P("pipe", None),
            P("pipe", None, None),
            P("pipe", None, "expert"),
            P("pipe", None, "expert"),
            P("pipe", "expert", None),
            P(None, "pipe", "expert", None),
            P(None, "pipe", "expert", None),
        ),
        out_specs=(P(None, "pipe", "expert", None), P(None, "pipe", "expert", None)),
        check_vma=False,
    )
```

time: 490 us -> 171 us (0.35); the launches traced: 481 us -> 169 us
  waiting for transfers between devices: 353 us -> 0 us
  Pallas kernels: 0 us -> 164 us
  other arithmetic: 51.5 us -> 0 us
  matrix products: 27.1 us -> 0 us
  blocking collectives: 25.1 us -> 0 us
  between operations: 14.9 us -> 0.66 us
  starting transfers between devices: 8.56 us -> 0 us
    reduce_scatter x4 -> x0, waiting for transfers between devices: 243 us -> none  [layer(): lax.psum_scatter(part, 'expert', scatter_dimension=0, tiled=True)]
    pallas_call x0 -> x1, Pallas kernels: none -> 164 us  [shards(): pl.pallas_call(functools.partial(relay_kernel, chips, sections), out_shap...]
    all_gather x4 -> x0, waiting for transfers between devices: 105 us -> none  [layer(): everyone = lax.all_gather(normed, 'expert', axis=0, tiled=True)]
    eq x1 -> x0, other arithmetic: 38.5 us -> none  [layer(): hidden = jnp.where(all_routes == mine, hidden, 0.0).astype(jnp.bfloat16)]
    dot_general x12 -> x0, matrix products: 27.1 us -> none  [the longest x4 13.7 us: layer(): acts = jnp.dot(everyone, both, preferred_element_type=jnp.float32)]
    all_gather x1 -> x0, blocking collectives: 25.1 us -> none  [shards(): all_routes = lax.all_gather(routes, 'expert', axis=2, tiled=True)]
    ppermute x2 -> x0, starting transfers between devices: 8.23 us -> none  [passed_along(): return lax.ppermute(block, axis, route)]
    convert_element_type x4 -> x0, other arithmetic: 5.09 us -> none  [the longest x2 2.93 us: normalize(): return (widened * inverse * gains[None, :]).astype(jnp.bfloat16)]
  transfers between devices with their start and end apart: 10 -> 0, of which waited for: 8 -> 0; matrix products, arithmetic and copies ran while one was open for 15% -> 0% of each run, Pallas kernels for 0% -> 0%
where the time goes in v2:
time: 171 us; the launch traced here: 169 us
  Pallas kernels  164 us (96%)
  local copies, waits for them, and re-layouts  4.73 us (3%)
    pallas_call x1, Pallas kernels, shards(): pl.pallas_call(functools.partial(relay_kernel, chips, sections), out_shap...  164 us

profile of v2, /device:TPU:6, one launch (start us, length us, event | category | flops | bytes accessed | tf_op | source)
XLA Modules:
  0.0 169.5 jit_solution(1360559951459654421)
XLA Ops:
  0.6 0.0 copy-start.1
  0.6 0.7 copy-done.1
  1.3 0.0 copy-start.2
  1.3 0.7 copy.13.first_routes
  2.0 0.0 copy-done.2
  2.0 0.7 copy.14.second_routes
  2.7 164.1 %relay_window.1 = (bf16[2,32,3584]{2,1,0:T(8,128)(2,1)}, bf16[2,32,3584]{2,1,0:T(8,128)(2,1)}) custom-call(bf16[1,32,3584]{2,1,0:T(8,128)(2,1)} %first_state.1, bf16[1,32,3584]{2,1,0:T(8,128)(2,1)} %second_state.1, bf16[1,32,3584]{2,1,0:T(8,128)(2,1)} %first_enter.1, bf16[1,32,3584]{2,1,0:T(8,128)(2,1)} %second_enter.1, f32[1,3584]{1,0:T(1,128)} %gains.1, ...), custom_call_target="tpu_custom_call" | custom-call | tf_op jit(solution)/shard_map/relay_window/pallas_call | solution.py:415
  166.8 0.0 copy-start
  166.8 1.9 %copy.19 = bf16[2,1,32,3584]{3,2,1,0:T(8,128)(2,1)} copy(bf16[2,1,32,3584]{3,2,1,0:T(8,128)(2,1)} %bitcast.18) | data formatting | bytes 917504
  168.7 0.0 copy-done
  168.7 0.8 copy.20
Async XLA Ops:
  0.6 0.7 copy-start.1
  1.3 0.7 copy-start.2
  166.8 1.9 %copy-start = (bf16[2,32,3584]{2,1,0:T(8,128)(2,1)S(1)}, bf16[2,32,3584]{2,1,0:T(8,128)(2,1)}, u32[]{:S(2)}) copy-start(bf16[2,32,3584]{2,1,0:T(8,128)(2,1)} %get-tuple-element.5) | copy-start | bytes 1376260

commit v3 on v1

v3 whole, which is shorter than its diff:
```python
import functools

import jax
import jax.numpy as jnp
from jax import lax
from jax.experimental import pallas as pl
from jax.experimental.pallas import tpu as pltpu
from jax.sharding import PartitionSpec as P

EXP_WIN = 2
MESH = pl.DeviceIdType.MESH

epsilon = 1e-06
route_scale = 2.5

LANES = 128
FOLD = 256
REACH = 5
PIECES = 2


ORDER = (
    ("prepare", 0, 0),
    ("start", 0, 0),
    ("gather", 0, 0, 1, 0),
    ("prepare", 0, 1),
    ("gather", 0, 0, 1, 1),
    ("start", 0, 1),
    ("gather", 0, 0, 2, 0),
    ("gather", 0, 0, 2, 1),
    ("gather", 0, 1, 1, 0),
    ("gather", 0, 0, 3, 0),
    ("gather", 0, 1, 1, 1),
    ("gather", 0, 0, 3, 1),
    ("gather", 0, 1, 2, 0),
    ("gather", 0, 0, 4, 0),
    ("gather", 0, 0, 4, 1),
    ("gather", 0, 1, 2, 1),
    ("gather", 0, 1, 3, 0),
    ("gather", 0, 0, 5, 0),
    ("gather", 0, 0, 5, 1),
    ("compute", 0, 0),
    ("gather", 0, 1, 3, 1),
    ("total", 0, 0, 5),
    ("gather", 0, 1, 4, 0),
    ("gather", 0, 1, 4, 1),
    ("gather", 0, 1, 5, 0),
    ("total", 0, 0, 4),
    ("reduce", 0, 0, 1, 0),
    ("reduce", 0, 0, 1, 1),
    ("gather", 0, 1, 5, 1),
    ("total", 0, 0, 3),
    ("reduce", 0, 0, 2, 0),
    ("reduce", 0, 0, 2, 1),
    ("compute", 0, 1),
    ("total", 0, 1, 5),
    ("total", 0, 0, 2),
    ("reduce", 0, 0, 3, 0),
    ("reduce", 0, 0, 3, 1),
    ("total", 0, 0, 1),
    ("total", 0, 1, 4),
    ("reduce", 0, 1, 1, 0),
    ("reduce", 0, 0, 4, 0),
    ("reduce", 0, 1, 1, 1),
    ("reduce", 0, 0, 4, 1),
    ("total", 0, 1, 3),
    ("reduce", 0, 1, 2, 0),
    ("reduce", 0, 0, 5, 0),
    ("reduce", 0, 1, 2, 1),
    ("reduce", 0, 0, 5, 1),
    ("finish", 0, 0, 0),
    ("finish", 0, 0, 1),
    ("total", 0, 1, 2),
    ("reduce", 0, 1, 3, 0),
    ("reduce", 0, 1, 3, 1),
    ("total", 0, 1, 1),
    ("reduce", 0, 1, 4, 0),
    ("reduce", 0, 1, 4, 1),
    ("prepare", 1, 0),
    ("reduce", 0, 1, 5, 0),
    ("reduce", 0, 1, 5, 1),
    ("finish", 0, 1, 0),
    ("start", 1, 0),
    ("finish", 0, 1, 1),
    ("gather", 1, 0, 1, 0),
    ("gather", 1, 0, 1, 1),
    ("gather", 1, 0, 2, 0),
    ("prepare", 1, 1),
    ("gather", 1, 0, 2, 1),
    ("start", 1, 1),
    ("gather", 1, 0, 3, 0),
    ("gather", 1, 1, 1, 0),
    ("gather", 1, 1, 1, 1),
    ("gather", 1, 0, 3, 1),
    ("gather", 1, 1, 2, 0),
    ("gather", 1, 0, 4, 0),
    ("gather", 1, 0, 4, 1),
    ("gather", 1, 1, 2, 1),
    ("gather", 1, 0, 5, 0),
    ("gather", 1, 0, 5, 1),
    ("compute", 1, 0),
    ("total", 1, 0, 5),
    ("gather", 1, 1, 3, 0),
    ("total", 1, 0, 4),
    ("gather", 1, 1, 3, 1),
    ("gather", 1, 1, 4, 0),
    ("gather", 1, 1, 4, 1),
    ("gather", 1, 1, 5, 0),
    ("reduce", 1, 0, 1, 0),
    ("reduce", 1, 0, 1, 1),
    ("total", 1, 0, 3),
    ("gather", 1, 1, 5, 1),
    ("compute", 1, 1),
    ("total", 1, 1, 5),
    ("reduce", 1, 0, 2, 0),
    ("total", 1, 1, 4),
    ("reduce", 1, 0, 2, 1),
    ("reduce", 1, 1, 1, 0),
    ("reduce", 1, 1, 1, 1),
    ("total", 1, 0, 2),
    ("total", 1, 1, 3),
    ("reduce", 1, 0, 3, 0),
    ("reduce", 1, 1, 2, 0),
    ("reduce", 1, 1, 2, 1),
    ("reduce", 1, 0, 3, 1),
    ("total", 1, 1, 2),
    ("total", 1, 0, 1),
    ("reduce", 1, 1, 3, 0),
    ("reduce", 1, 1, 3, 1),
    ("reduce", 1, 0, 4, 0),
    ("total", 1, 1, 1),
    ("reduce", 1, 1, 4, 0),
    ("reduce", 1, 1, 4, 1),
    ("reduce", 1, 0, 4, 1),
    ("reduce", 1, 0, 5, 0),
    ("reduce", 1, 1, 5, 0),
    ("reduce", 1, 1, 5, 1),
    ("finish", 1, 1, 0),
    ("reduce", 1, 0, 5, 1),
    ("finish", 1, 1, 1),
    ("finish", 1, 0, 0),
    ("finish", 1, 0, 1),
)


def relay_kernel(
    chips,
    sections,
    first_state,
    second_state,
    first_enter,
    second_enter,
    gains,
    router,
    gate_hbm,
    up_hbm,
    down_hbm,
    first_routes,
    second_routes,
    first_out,
    second_out,
    held,
    other,
    part,
    sums,
    other_sum,
    arrived,
    current,
    weight,
    both,
    down,
    fold,
    outcome,
    extra_in,
    extra_out,
    fold_sum,
    g_s,
    g_r,
    r_s,
    r_r,
    share_s,
    share_r,
    pipe_s,
    pipe_r,
    load_sem,
):
    rows, width = current.shape[1:]
    half_rows = rows // 2
    units = gate_hbm.shape[1]
    folds = width // LANES
    piece = (width + FOLD) // PIECES
    group = chips // EXP_WIN
    e = lax.axis_index("expert")
    p = lax.axis_index("pipe")
    z, c = e // 2, e % 2
    own_expert = (z // group).astype(jnp.float32)
    above = {"expert": ((z + 1) % chips) * 2 + c}
    below = {"expert": ((z + chips - 1) % chips) * 2 + c}
    sibling = {"expert": z * 2 + (1 - c)}
    further = (
        {"expert": ((z + chips - 2) % chips) * 2 + c},
        {"expert": ((z + 2) % chips) * 2 + c},
    )
    onward = {"pipe": (p + 1) % sections}
    backward = {"pipe": (p + sections - 1) % sections}
    nexts = (below, above)
    ranks = (z % group, group - 1 - z % group)
    routes = (first_routes, second_routes)
    states = (first_state, second_state)
    enters = (first_enter, second_enter)
    outs = (first_out, second_out)

    def ahead(way, distance):
        return (z + (chips - distance if way == 0 else distance)) % chips

    def behind(way, distance):
        return ahead(1 - way, distance)

    def remote(src, dst, send, recv, device):
        return pltpu.make_async_remote_copy(
            src_ref=src,
            dst_ref=dst,
            send_sem=send,
            recv_sem=recv,
            device_id=device,
            device_id_type=MESH,
        )

    def columns(h):
        return pl.ds(h * piece, piece)

    def gather_copy(t, s, way, src, chip, index, h, device):
        return remote(
            src.at[:, columns(h)],
            held.at[t, s, chip, :, columns(h)],
            g_s.at[way, t, s, index, h],
            g_r.at[way, t, s, index, h],
            device,
        )

    def gather_own(t, s, way, h):
        return gather_copy(t, s, way, held.at[t, s, z], z, 1, h, nexts[way])

    def gather_other(t, s, way, h):
        return gather_copy(t, s, way, other.at[t, s], z, 1, h, nexts[way])

    def gather_further(t, s, way, h):
        return gather_copy(t, s, way, other.at[t, s], z, 2, h, further[way])

    def gather_forward(t, s, way, d, h):
        chip = behind(way, d)
        return gather_copy(t, s, way, held.at[t, s, chip], chip, d + 1, h, nexts[way])

    def gather_arrival(t, s, way, d, h):
        chip = behind(way, d)
        return gather_copy(t, s, way, held.at[t, s, chip], chip, d, h, nexts[way])

    def start_gather(t, s):
        for h in range(PIECES):
            for way, rank in enumerate(ranks):

                @pl.when(rank == 1)
                def _():
                    gather_further(t, s, way, h).start()

                @pl.when(rank == 0)
                def _():
                    gather_other(t, s, way, h).start()

                @pl.when(rank >= 1)
                def _():
                    gather_own(t, s, way, h).start()

    def gather_step(t, s, d, h):
        for way, rank in enumerate(ranks):

            @pl.when(rank <= REACH - d)
            def _():
                gather_arrival(t, s, way, d, h).wait_recv()
                if d < REACH:

                    @pl.when(rank >= 1)
                    def _():
                        gather_forward(t, s, way, d, h).start()

    def finish_gather(t, s):
        for h in range(PIECES):
            for way, rank in enumerate(ranks):

                @pl.when(rank == 1)
                def _():
                    gather_further(t, s, way, h).wait_send()

                @pl.when(rank == 0)
                def _():
                    gather_other(t, s, way, h).wait_send()

                @pl.when(rank >= 1)
                def _():
                    gather_own(t, s, way, h).wait_send()

                for d in range(1, REACH):

                    @pl.when((rank <= REACH - d) & (rank >= 1))
                    def _():
                        gather_forward(t, s, way, d, h).wait_send()

    def share_copies():
        own, theirs = pl.ds(0, units), pl.ds(units, units)
        targets = (
            (gate_hbm, both.at[:, theirs]),
            (up_hbm, both.at[:, pl.ds(3 * units, units)]),
            (down_hbm, down.at[theirs]),
        )
        return [
            remote(src, dst, share_s.at[i], share_r.at[i], sibling)
            for i, (src, dst) in enumerate(targets)
        ]

    def place(k):
        return (k % half_rows), pl.ds((k // half_rows) * LANES, LANES)

    def compute(t, s):
        count = chips * half_rows
        along = lax.broadcasted_iota(jnp.int32, (count, count), 0)
        across = lax.broadcasted_iota(jnp.int32, (count, count), 1)

        def turning(inner, outer):
            onehot = across == (along % outer) * inner + along // outer
            return onehot.astype(jnp.float32).astype(jnp.bfloat16)

        folded = held[t, s, :, :, 0:FOLD].reshape(count, FOLD)
        turned = jnp.dot(
            turning(half_rows, chips), folded, preferred_element_type=jnp.float32
        )
        for k in range(folds):
            row, lanes = place(k)
            start = (k // half_rows) * LANES
            extra_in[0:chips, k * LANES : (k + 1) * LANES] = turned[
                row * chips : (row + 1) * chips, start : start + LANES
            ]
        tokens = held[t, s, :, :, FOLD : FOLD + width].reshape(count, width)
        tokens = jnp.concatenate([tokens, extra_in[...].astype(jnp.bfloat16)], axis=0)
        acts = jnp.dot(tokens, both[...], preferred_element_type=jnp.float32)
        gate_act, up_act = acts[:, : 2 * units], acts[:, 2 * units :]
        hidden = (gate_act * jax.nn.sigmoid(gate_act) * up_act).astype(jnp.bfloat16)
        step = 2 * LANES
        for start in range(0, width, step):
            product = jnp.dot(
                hidden, down[:, pl.ds(start, step)], preferred_element_type=jnp.float32
            )
            for k in range(start // LANES, (start + step) // LANES):
                row, lanes = place(k)
                at = k * LANES - start
                extra_out[row * chips : (row + 1) * chips, lanes] = product[
                    count : count + chips, at : at + LANES
                ]
            product = product[:count].astype(jnp.bfloat16).reshape(chips, half_rows, step)
            part[t, s, :, :, pl.ds(FOLD + start, step)] = product
        folded = jnp.dot(
            turning(chips, half_rows),
            extra_out[...].astype(jnp.bfloat16),
            preferred_element_type=jnp.float32,
        )
        part[t, s, :, :, 0:FOLD] = folded.astype(jnp.bfloat16).reshape(chips, half_rows, FOLD)

    def reduce_copy(t, s, way, d, h, dst, index, device):
        return remote(
            part.at[t, s, ahead(way, d), :, columns(h)],
            dst.at[:, columns(h)],
            r_s.at[way, t, s, index, h],
            r_r.at[way, t, s, index, h],
            device,
        )

    def reduce_on(t, s, way, d, h):
        return reduce_copy(t, s, way, d, h, sums.at[way, t, s, d - 1], d - 1, nexts[way])

    def reduce_out(t, s, way, d, h):
        device = nexts[way] if d == 1 else further[way]
        return reduce_copy(t, s, way, d, h, other_sum.at[t, s], REACH, device)

    def add_up(t, s, way, d, h):
        home, cols = ahead(way, d), columns(h)
        total = part[t, s, home, :, cols].astype(jnp.float32)
        total = total + sums[way, t, s, d, :, cols].astype(jnp.float32)
        part[t, s, home, :, cols] = total.astype(jnp.bfloat16)

    def start_reduce(t, s, d):
        for way, rank in enumerate(ranks):

            @pl.when(rank == group - 1)
            def _():
                for h in range(PIECES):
                    reduce_on(t, s, way, d, h).start()

    def reduce_step(t, s, r, h):
        d = REACH - r
        for way, rank in enumerate(ranks):

            @pl.when((rank >= d - 2) & (rank < group - 1))
            def _():
                reduce_on(t, s, way, d + 1, h).wait_recv()
                if d >= 1:
                    add_up(t, s, way, d, h)

                    @pl.when(rank >= 1)
                    def _():
                        reduce_on(t, s, way, d, h).start()

                    if d <= 2:

                        @pl.when(rank == 0)
                        def _():
                            reduce_out(t, s, way, d, h).start()

            if d == 0:

                @pl.when(rank >= group - 2)
                def _():
                    reduce_out(t, s, way, 1, h).wait_recv()

    def finish_reduce(t, s):
        for h in range(PIECES):
            for way, rank in enumerate(ranks):

                @pl.when(rank == group - 1)
                def _():
                    for d in range(REACH, 0, -1):
                        reduce_on(t, s, way, d, h).wait_send()

                for d in range(1, REACH):

                    @pl.when((rank >= d - 2) & (rank < group - 1) & (rank >= 1))
                    def _():
                        reduce_on(t, s, way, d, h).wait_send()

                @pl.when(rank == 0)
                def _():
                    reduce_out(t, s, way, 2, h).wait_send()
                    reduce_out(t, s, way, 1, h).wait_send()

    def packing(t, s):
        along = lax.broadcasted_iota(jnp.int32, (rows, rows), 0)
        across = lax.broadcasted_iota(jnp.int32, (rows, rows), 1)

        def column(row):
            spread = jnp.broadcast_to(row, (rows, rows))
            return jnp.sum(jnp.where(across == along, spread, 0.0), axis=1, keepdims=True)

        named = routes[s][t].astype(jnp.float32)
        away = jnp.abs(named - own_expert)
        before = jnp.where(along < across, jnp.broadcast_to(column(away), (rows, rows)), 0.0)
        before = jnp.sum(before, axis=0, keepdims=True)
        index = lax.broadcasted_iota(jnp.int32, (1, rows), 1).astype(jnp.float32)
        order = jnp.where(away > 0.5, before, index - before)
        spare = jnp.where(away > 0.5, half_rows - 1.0, rows - 1.0)
        put = jnp.where(order < half_rows, order + half_rows * away, spare)
        return along, across, named, put, column(put), jnp.sum(away, axis=1, keepdims=True)

    def prepare(t, s):
        along, across, named, put, _, _ = packing(t, s)
        onehot = (along.astype(jnp.float32) == put).astype(jnp.float32)
        chosen = jnp.sum(onehot * named, axis=1, keepdims=True)
        packed = jnp.dot(
            onehot.astype(jnp.bfloat16), current[s], preferred_element_type=jnp.float32
        )
        current[s] = packed.astype(jnp.bfloat16)
        for h in range(2):
            widened = packed[h * half_rows : (h + 1) * half_rows]
            mean = jnp.mean(widened * widened, axis=-1, keepdims=True)
            normed = widened * lax.rsqrt(mean + epsilon) * gains[...]
            normed = normed.astype(jnp.bfloat16)
            if h == 0:
                held[t, s, z, :, FOLD : FOLD + width] = normed
            else:
                other[t, s, :, FOLD : FOLD + width] = normed
            normed = normed.astype(jnp.float32)
            for k in range(folds):
                row, lanes = place(k)
                fold[1 - h, row : row + 1, lanes] = normed[
                    half_rows - 1 : half_rows, k * LANES : (k + 1) * LANES
                ]
            part_of = chosen[h * half_rows : (h + 1) * half_rows]
            column = jnp.where(part_of < 0.5, router[0:1], router[1:2])
            score = jnp.sum(normed * column, axis=1, keepdims=True)
            weight[s, h * half_rows : (h + 1) * half_rows] = jnp.broadcast_to(
                route_scale * jax.nn.sigmoid(score), (half_rows, LANES)
            )
        held[t, s, z, :, 0:FOLD] = fold[0].astype(jnp.bfloat16)
        other[t, s, :, 0:FOLD] = fold[1].astype(jnp.bfloat16)

    def main_columns(h):
        first = max(h * piece, FOLD) - FOLD
        return first, (h + 1) * piece - FOLD

    def pipe_copy(s, h):
        first, last = main_columns(h)
        cols = pl.ds(first, last - first)
        return remote(
            outs[s].at[0, :, cols],
            arrived.at[s, :, cols],
            pipe_s.at[s, h],
            pipe_r.at[s, h],
            onward if s == 0 else backward,
        )

    def receive(s):
        for h in range(PIECES):
            pipe_copy(s, h).wait_recv()
        current[s] = arrived[s]

        @pl.when(p == (0 if s == 0 else sections - 1))
        def _():
            current[s] = enters[s][0]

    def finalize(t, s, h):
        _, across, _, _, put, load = packing(t, s)
        first, last = main_columns(h)

        def sums_of(cols):
            total = part[t, s, z, :, cols].astype(jnp.float32)
            total = total + sums[0, t, s, 0, :, cols].astype(jnp.float32)
            total = total + sums[1, t, s, 0, :, cols].astype(jnp.float32)
            return total, other_sum[t, s, :, cols].astype(jnp.float32)

        if h == 0:
            fold_sum[0], fold_sum[1] = sums_of(pl.ds(0, FOLD))
        crowded = (load > half_rows + 0.5, load < half_rows - 0.5)
        both_sums = sums_of(pl.ds(FOLD + first, last - first))
        for b in range(2):
            outcome[b * half_rows : (b + 1) * half_rows, first:last] = both_sums[b]
            end = (b + 1) * half_rows - 1
            for k in range(first // LANES, last // LANES):
                row, lanes = place(k)
                here = pl.ds(k * LANES, LANES)
                outcome[end : end + 1, here] = jnp.where(
                    crowded[b], fold_sum[1 - b, row : row + 1, lanes], outcome[end : end + 1, here]
                )
        widened = current[s, :, first:last].astype(jnp.float32)
        result = widened + weight[s, :, 0:1] * outcome[:, first:last]
        back = (across.astype(jnp.float32) == put).astype(jnp.float32).astype(jnp.bfloat16)
        result = jnp.dot(back, result.astype(jnp.bfloat16), preferred_element_type=jnp.float32)
        outs[s][t, :, first:last] = result.astype(jnp.bfloat16)
        if t == 0:
            pipe_copy(s, h).start()

    barrier = pltpu.get_barrier_semaphore()
    partners = (above, below, sibling, onward, backward) + further
    for partner in partners:
        pl.semaphore_signal(barrier, inc=1, device_id=partner, device_id_type=MESH)
    loads = (
        pltpu.make_async_copy(gate_hbm, both.at[:, pl.ds(0, units)], load_sem.at[0]),
        pltpu.make_async_copy(up_hbm, both.at[:, pl.ds(2 * units, units)], load_sem.at[1]),
        pltpu.make_async_copy(down_hbm, down.at[pl.ds(0, units)], load_sem.at[2]),
    )
    for load in loads:
        load.start()
    fold[...] = jnp.zeros_like(fold)
    extra_in[...] = jnp.zeros_like(extra_in)
    extra_out[...] = jnp.zeros_like(extra_out)
    for way, rank in enumerate(ranks):

        @pl.when(rank == group - 1)
        def _():
            for t in range(2):
                for s in range(2):
                    sums[way, t, s, 0] = jnp.zeros_like(sums[way, t, s, 0])

    entered = []
    for step, t, s, *at in ORDER:
        if step == "prepare":
            if t == 0:
                current[s] = states[s][0]
            else:
                receive(s)
            prepare(t, s)
        elif step == "start":
            if not entered:
                pl.semaphore_wait(barrier, len(partners))
            start_gather(t, s)
            if not entered:
                for copy in share_copies():
                    copy.start()
            entered.append(step)
        elif step == "gather":
            gather_step(t, s, *at)
        elif step == "compute":
            if (t, s) == (0, 0):
                for load in loads:
                    load.wait()
                for copy in share_copies():
                    copy.wait()
            compute(t, s)
        elif step == "total":
            start_reduce(t, s, *at)
        elif step == "reduce":
            reduce_step(t, s, *at)
        else:
            finalize(t, s, *at)
    for s in range(2):
        for t in range(2):
            finish_gather(t, s)
            finish_reduce(t, s)
        for h in range(PIECES):
            pipe_copy(s, h).wait_send()


def shards(
    first_state,
    second_state,
    first_enter,
    second_enter,
    norm_gain,
    router,
    gate_proj,
    up_proj,
    down_proj,
    first_routes,
    second_routes,
):
    chips = lax.axis_size("expert") // 2
    sections = lax.axis_size("pipe")
    rows, width = first_state.shape[1:]
    half_rows, across = rows // 2, width + FOLD
    units = gate_proj.shape[2]
    steps = first_routes.shape[0]
    vmem = pl.BlockSpec(memory_space=pltpu.VMEM)
    hbm = pl.BlockSpec(memory_space=pl.ANY)
    bf16 = jnp.bfloat16
    dma = pltpu.SemaphoreType.DMA
    out = jax.ShapeDtypeStruct((steps, rows, width), bf16)
    outs = pl.pallas_call(
        functools.partial(relay_kernel, chips, sections),
        out_shape=(out, out),
        in_specs=[vmem] * 6 + [hbm] * 3 + [vmem] * 2,
        out_specs=(vmem, vmem),
        scratch_shapes=[
            pltpu.VMEM((steps, 2, chips, half_rows, across), bf16),
            pltpu.VMEM((steps, 2, half_rows, across), bf16),
            pltpu.VMEM((steps, 2, chips, half_rows, across), bf16),
            pltpu.VMEM((2, steps, 2, REACH, half_rows, across), bf16),
            pltpu.VMEM((steps, 2, half_rows, across), bf16),
            pltpu.VMEM((2, rows, width), bf16),
            pltpu.VMEM((2, rows, width), bf16),
            pltpu.VMEM((2, rows, LANES), jnp.float32),
            pltpu.VMEM((width, 4 * units), bf16),
            pltpu.VMEM((2 * units, width), bf16),
            pltpu.VMEM((2, half_rows, FOLD), jnp.float32),
            pltpu.VMEM((rows, width), jnp.float32),
            pltpu.VMEM((2 * chips, width), jnp.float32),
            pltpu.VMEM((chips * half_rows, FOLD), jnp.float32),
            pltpu.VMEM((2, half_rows, FOLD), jnp.float32),
        ]
        + [dma((2, steps, 2, REACH + 1, PIECES))] * 4
        + [dma((3,))] * 2
        + [dma((2, PIECES))] * 2
        + [dma((3,))],
        compiler_params=pltpu.CompilerParams(
            collective_id=0, has_side_effects=True, vmem_limit_bytes=60 << 20
        ),
        name="relay_window",
    )(
        first_state,
        second_state,
        first_enter,
        second_enter,
        norm_gain,
        router[0].T,
        gate_proj[0],
        up_proj[0],
        down_proj[0],
        first_routes.reshape(steps, 1, rows),
        second_routes.reshape(steps, 1, rows),
    )
    return (outs[0][:, None], outs[1][:, None])


def solution(mesh):
    return jax.shard_map(
        shards,
        mesh=mesh,
        in_specs=(
            P("pipe", "expert", None),
            P("pipe", "expert", None),
            P(None, "expert", None),
            P(None, "expert", None),
            P("pipe", None),
            P("pipe", None, None),
            P("pipe", None, "expert"),
            P("pipe", None, "expert"),
            P("pipe", "expert", None),
            P(None, "pipe", "expert", None),
            P(None, "pipe", "expert", None),
        ),
        out_specs=(P(None, "pipe", "expert", None), P(None, "pipe", "expert", None)),
        check_vma=False,
    )
```

time: 490 us -> 146 us (0.30); the launches traced: 481 us -> 146 us
  waiting for transfers between devices: 353 us -> 0 us
  Pallas kernels: 0 us -> 143 us
  other arithmetic: 51.5 us -> 0 us
  matrix products: 27.1 us -> 0 us
  blocking collectives: 25.1 us -> 0 us
  between operations: 14.9 us -> 0.65 us
  starting transfers between devices: 8.56 us -> 0 us
    reduce_scatter x4 -> x0, waiting for transfers between devices: 243 us -> none  [layer(): lax.psum_scatter(part, 'expert', scatter_dimension=0, tiled=True)]
    pallas_call x0 -> x1, Pallas kernels: none -> 143 us  [shards(): pl.pallas_call(functools.partial(relay_kernel, chips, sections), out_shap...]
    all_gather x4 -> x0, waiting for transfers between devices: 105 us -> none  [layer(): everyone = lax.all_gather(normed, 'expert', axis=0, tiled=True)]
    eq x1 -> x0, other arithmetic: 38.5 us -> none  [layer(): hidden = jnp.where(all_routes == mine, hidden, 0.0).astype(jnp.bfloat16)]
    dot_general x12 -> x0, matrix products: 27.1 us -> none  [the longest x4 13.7 us: layer(): acts = jnp.dot(everyone, both, preferred_element_type=jnp.float32)]
    all_gather x1 -> x0, blocking collectives: 25.1 us -> none  [shards(): all_routes = lax.all_gather(routes, 'expert', axis=2, tiled=True)]
    ppermute x2 -> x0, starting transfers between devices: 8.23 us -> none  [passed_along(): return lax.ppermute(block, axis, route)]
    convert_element_type x4 -> x0, other arithmetic: 5.09 us -> none  [the longest x2 2.93 us: normalize(): return (widened * inverse * gains[None, :]).astype(jnp.bfloat16)]
  transfers between devices with their start and end apart: 10 -> 0, of which waited for: 8 -> 0; matrix products, arithmetic and copies ran while one was open for 15% -> 0% of each run, Pallas kernels for 0% -> 0%
where the time goes in v3:
time: 146 us
  Pallas kernels  143 us (98%)
  local copies, waits for them, and re-layouts  2.64 us (2%)
    pallas_call x1, Pallas kernels, shards(): pl.pallas_call(functools.partial(relay_kernel, chips, sections), out_shap...  143 us

profile of v3, /device:TPU:6, one launch (start us, length us, event | category | flops | bytes accessed | tf_op | source)
XLA Modules:
  0.0 146.1 jit_solution(1968215034743996426)
XLA Ops:
  0.6 142.8 %relay_window.1 = (bf16[2,32,3584]{2,1,0:T(8,128)(2,1)}, bf16[2,32,3584]{2,1,0:T(8,128)(2,1)}) custom-call(bf16[1,32,3584]{2,1,0:T(8,128)(2,1)} %first_state.1, bf16[1,32,3584]{2,1,0:T(8,128)(2,1)} %second_state.1, bf16[1,32,3584]{2,1,0:T(8,128)(2,1)} %first_enter.1, bf16[1,32,3584]{2,1,0:T(8,128)(2,1)} %second_enter.1, f32[1,3584]{1,0:T(1,128)} %gains.1, ...), custom_call_target="tpu_custom_call" | custom-call | tf_op jit(solution)/shard_map/relay_window/pallas_call | solution.py:633
  143.5 0.0 copy-start
  143.5 1.9 %copy.19 = bf16[2,1,32,3584]{3,2,1,0:T(8,128)(2,1)} copy(bf16[2,1,32,3584]{3,2,1,0:T(8,128)(2,1)} %bitcast.22) | data formatting | bytes 917504
  145.4 0.0 copy-done
  145.4 0.8 copy.20
Async XLA Ops:
  143.5 1.9 %copy-start = (bf16[2,32,3584]{2,1,0:T(8,128)(2,1)S(1)}, bf16[2,32,3584]{2,1,0:T(8,128)(2,1)}, u32[]{:S(2)}) copy-start(bf16[2,32,3584]{2,1,0:T(8,128)(2,1)} %get-tuple-element.5) | copy-start | bytes 1376260

commit v4 on v3

--- a/solution.py
+++ b/solution.py
@@ -17,129 +17,207 @@
 FOLD = 256
 REACH = 5
 PIECES = 2
-
+BATCHES = ((-2, -1, 0, 1, 2), (3, 4, 5))
+
+
+PREPARE, START, GATHER, COMPUTE, TOTAL, REDUCE, OUTSIDE, SENT, FINISH = range(9)
 
 ORDER = (
-    ("prepare", 0, 0),
-    ("start", 0, 0),
-    ("gather", 0, 0, 1, 0),
-    ("prepare", 0, 1),
-    ("gather", 0, 0, 1, 1),
-    ("start", 0, 1),
-    ("gather", 0, 0, 2, 0),
-    ("gather", 0, 0, 2, 1),
-    ("gather", 0, 1, 1, 0),
-    ("gather", 0, 0, 3, 0),
-    ("gather", 0, 1, 1, 1),
-    ("gather", 0, 0, 3, 1),
-    ("gather", 0, 1, 2, 0),
-    ("gather", 0, 0, 4, 0),
-    ("gather", 0, 0, 4, 1),
-    ("gather", 0, 1, 2, 1),
-    ("gather", 0, 1, 3, 0),
-    ("gather", 0, 0, 5, 0),
-    ("gather", 0, 0, 5, 1),
-    ("compute", 0, 0),
-    ("gather", 0, 1, 3, 1),
-    ("total", 0, 0, 5),
-    ("gather", 0, 1, 4, 0),
-    ("gather", 0, 1, 4, 1),
-    ("gather", 0, 1, 5, 0),
-    ("total", 0, 0, 4),
-    ("reduce", 0, 0, 1, 0),
-    ("reduce", 0, 0, 1, 1),
-    ("gather", 0, 1, 5, 1),
-    ("total", 0, 0, 3),
-    ("reduce", 0, 0, 2, 0),
-    ("reduce", 0, 0, 2, 1),
-    ("compute", 0, 1),
-    ("total", 0, 1, 5),
-    ("total", 0, 0, 2),
-    ("reduce", 0, 0, 3, 0),
-    ("reduce", 0, 0, 3, 1),
-    ("total", 0, 0, 1),
-    ("total", 0, 1, 4),
-    ("reduce", 0, 1, 1, 0),
-    ("reduce", 0, 0, 4, 0),
-    ("reduce", 0, 1, 1, 1),
-    ("reduce", 0, 0, 4, 1),
-    ("total", 0, 1, 3),
-    ("reduce", 0, 1, 2, 0),
-    ("reduce", 0, 0, 5, 0),
-    ("reduce", 0, 1, 2, 1),
-    ("reduce", 0, 0, 5, 1),
-    ("finish", 0, 0, 0),
-    ("finish", 0, 0, 1),
-    ("total", 0, 1, 2),
-    ("reduce", 0, 1, 3, 0),
-    ("reduce", 0, 1, 3, 1),
-    ("total", 0, 1, 1),
-    ("reduce", 0, 1, 4, 0),
-    ("reduce", 0, 1, 4, 1),
-    ("prepare", 1, 0),
-    ("reduce", 0, 1, 5, 0),
-    ("reduce", 0, 1, 5, 1),
-    ("finish", 0, 1, 0),
-    ("start", 1, 0),
-    ("finish", 0, 1, 1),
-    ("gather", 1, 0, 1, 0),
-    ("gather", 1, 0, 1, 1),
-    ("gather", 1, 0, 2, 0),
-    ("prepare", 1, 1),
-    ("gather", 1, 0, 2, 1),
-    ("start", 1, 1),
-    ("gather", 1, 0, 3, 0),
-    ("gather", 1, 1, 1, 0),
-    ("gather", 1, 1, 1, 1),
-    ("gather", 1, 0, 3, 1),
-    ("gather", 1, 1, 2, 0),
-    ("gather", 1, 0, 4, 0),
-    ("gather", 1, 0, 4, 1),
-    ("gather", 1, 1, 2, 1),
-    ("gather", 1, 0, 5, 0),
-    ("gather", 1, 0, 5, 1),
-    ("compute", 1, 0),
-    ("total", 1, 0, 5),
-    ("gather", 1, 1, 3, 0),
-    ("total", 1, 0, 4),
-    ("gather", 1, 1, 3, 1),
-    ("gather", 1, 1, 4, 0),
-    ("gather", 1, 1, 4, 1),
-    ("gather", 1, 1, 5, 0),
-    ("reduce", 1, 0, 1, 0),
-    ("reduce", 1, 0, 1, 1),
-    ("total", 1, 0, 3),
-    ("gather", 1, 1, 5, 1),
-    ("compute", 1, 1),
-    ("total", 1, 1, 5),
-    ("reduce", 1, 0, 2, 0),
-    ("total", 1, 1, 4),
-    ("reduce", 1, 0, 2, 1),
-    ("reduce", 1, 1, 1, 0),
-    ("reduce", 1, 1, 1, 1),
-    ("total", 1, 0, 2),
-    ("total", 1, 1, 3),
-    ("reduce", 1, 0, 3, 0),
-    ("reduce", 1, 1, 2, 0),
-    ("reduce", 1, 1, 2, 1),
-    ("reduce", 1, 0, 3, 1),
-    ("total", 1, 1, 2),
-    ("total", 1, 0, 1),
-    ("reduce", 1, 1, 3, 0),
-    ("reduce", 1, 1, 3, 1),
-    ("reduce", 1, 0, 4, 0),
-    ("total", 1, 1, 1),
-    ("reduce", 1, 1, 4, 0),
-    ("reduce", 1, 1, 4, 1),
-    ("reduce", 1, 0, 4, 1),
-    ("reduce", 1, 0, 5, 0),
-    ("reduce", 1, 1, 5, 0),
-    ("reduce", 1, 1, 5, 1),
-    ("finish", 1, 1, 0),
-    ("reduce", 1, 0, 5, 1),
-    ("finish", 1, 1, 1),
-    ("finish", 1, 0, 0),
-    ("finish", 1, 0, 1),
+    (PREPARE, 0, 0),
+    (START, 0, 0),
+    (PREPARE, 0, 1),
+    (GATHER, 0, 0, 1, 0),
+    (GATHER, 0, 0, 1, 1),
+    (START, 0, 1),
+    (GATHER, 0, 0, 2, 0),
+    (GATHER, 0, 0, 2, 1),
+    (GATHER, 0, 1, 1, 0),
+    (COMPUTE, 0, 0, 0),
+    (GATHER, 0, 1, 1, 1),
+    (TOTAL, 0, 0, 1),
+    (TOTAL, 0, 0, 2),
+    (GATHER, 0, 0, 3, 0),
+    (GATHER, 0, 0, 3, 1),
+    (GATHER, 0, 1, 2, 0),
+    (GATHER, 0, 1, 2, 1),
+    (REDUCE, 0, 0, 1, 1, 0),
+    (COMPUTE, 0, 1, 0),
+    (REDUCE, 0, 0, 1, 1, 1),
+    (REDUCE, 0, 0, 2, 1, 0),
+    (TOTAL, 0, 1, 1),
+    (REDUCE, 0, 0, 2, 1, 1),
+    (TOTAL, 0, 1, 2),
+    (GATHER, 0, 0, 4, 0),
+    (GATHER, 0, 0, 4, 1),
+    (GATHER, 0, 1, 3, 0),
+    (GATHER, 0, 1, 3, 1),
+    (REDUCE, 0, 0, 2, 2, 0),
+    (REDUCE, 0, 1, 1, 1, 0),
+    (REDUCE, 0, 1, 1, 1, 1),
+    (REDUCE, 0, 1, 2, 1, 0),
+    (REDUCE, 0, 0, 2, 2, 1),
+    (GATHER, 0, 0, 5, 0),
+    (GATHER, 0, 0, 5, 1),
+    (REDUCE, 0, 1, 2, 1, 1),
+    (COMPUTE, 0, 0, 1),
+    (TOTAL, 0, 0, 5),
+    (TOTAL, 0, 0, 4),
+    (GATHER, 0, 1, 4, 0),
+    (GATHER, 0, 1, 4, 1),
+    (REDUCE, 0, 1, 2, 2, 0),
+    (SENT, 0, 0, GATHER),
+    (REDUCE, 0, 0, 5, 1, 0),
+    (REDUCE, 0, 0, 5, 1, 1),
+    (TOTAL, 0, 0, 3),
+    (REDUCE, 0, 1, 2, 2, 1),
+    (GATHER, 0, 1, 5, 0),
+    (GATHER, 0, 1, 5, 1),
+    (COMPUTE, 0, 1, 1),
+    (REDUCE, 0, 0, 4, 1, 0),
+    (REDUCE, 0, 0, 4, 1, 1),
+    (TOTAL, 0, 1, 5),
+    (REDUCE, 0, 0, 5, 2, 0),
+    (REDUCE, 0, 0, 5, 2, 1),
+    (REDUCE, 0, 0, 3, 1, 0),
+    (TOTAL, 0, 1, 4),
+    (REDUCE, 0, 0, 3, 1, 1),
+    (REDUCE, 0, 0, 4, 2, 0),
+    (REDUCE, 0, 0, 4, 2, 1),
+    (SENT, 0, 1, GATHER),
+    (REDUCE, 0, 1, 5, 1, 0),
+    (REDUCE, 0, 0, 5, 3, 0),
+    (REDUCE, 0, 1, 5, 1, 1),
+    (REDUCE, 0, 0, 5, 3, 1),
+    (TOTAL, 0, 1, 3),
+    (REDUCE, 0, 0, 3, 2, 0),
+    (REDUCE, 0, 0, 3, 2, 1),
+    (REDUCE, 0, 1, 4, 1, 0),
+    (REDUCE, 0, 0, 4, 3, 0),
+    (REDUCE, 0, 0, 4, 3, 1),
+    (REDUCE, 0, 0, 3, 3, 0),
+    (REDUCE, 0, 1, 4, 1, 1),
+    (REDUCE, 0, 1, 5, 2, 0),
+    (REDUCE, 0, 1, 5, 2, 1),
+    (REDUCE, 0, 0, 3, 3, 1),
+    (OUTSIDE, 0, 0, 0),
+    (OUTSIDE, 0, 0, 1),
+    (FINISH, 0, 0, 0),
+    (REDUCE, 0, 1, 3, 1, 0),
+    (REDUCE, 0, 1, 3, 1, 1),
+    (REDUCE, 0, 1, 4, 2, 0),
+    (REDUCE, 0, 1, 4, 2, 1),
+    (FINISH, 0, 0, 1),
+    (REDUCE, 0, 1, 5, 3, 0),
+    (REDUCE, 0, 1, 5, 3, 1),
+    (REDUCE, 0, 1, 3, 2, 0),
+    (REDUCE, 0, 1, 3, 2, 1),
+    (REDUCE, 0, 1, 4, 3, 0),
+    (REDUCE, 0, 1, 4, 3, 1),
+    (PREPARE, 1, 0),
+    (REDUCE, 0, 1, 3, 3, 0),
+    (REDUCE, 0, 1, 3, 3, 1),
+    (OUTSIDE, 0, 1, 0),
+    (OUTSIDE, 0, 1, 1),
+    (FINISH, 0, 1, 0),
+    (START, 1, 0),
+    (FINISH, 0, 1, 1),
+    (GATHER, 1, 0, 1, 0),
+    (GATHER, 1, 0, 1, 1),
+    (PREPARE, 1, 1),
+    (START, 1, 1),
+    (GATHER, 1, 0, 2, 0),
+    (GATHER, 1, 0, 2, 1),
+    (COMPUTE, 1, 0, 0),
+    (GATHER, 1, 1, 1, 0),
+    (GATHER, 1, 1, 1, 1),
+    (TOTAL, 1, 0, 1),
+    (TOTAL, 1, 0, 2),
+    (GATHER, 1, 1, 2, 0),
+    (GATHER, 1, 1, 2, 1),
+    (SENT, 0, 0, REDUCE),
+    (GATHER, 1, 0, 3, 0),
+    (GATHER, 1, 0, 3, 1),
+    (REDUCE, 1, 0, 1, 1, 0),
+    (REDUCE, 1, 0, 1, 1, 1),
+    (REDUCE, 1, 0, 2, 1, 0),
+    (COMPUTE, 1, 1, 0),
+    (TOTAL, 1, 1, 1),
+    (TOTAL, 1, 1, 2),
+    (SENT, 0, 1, REDUCE),
+    (GATHER, 1, 1, 3, 0),
+    (GATHER, 1, 1, 3, 1),
+    (REDUCE, 1, 0, 2, 1, 1),
+    (REDUCE, 1, 1, 1, 1, 0),
+    (GATHER, 1, 0, 4, 0),
+    (REDUCE, 1, 1, 1, 1, 1),
+    (GATHER, 1, 0, 4, 1),
+    (REDUCE, 1, 0, 2, 2, 0),
+    (REDUCE, 1, 1, 2, 1, 0),
+    (REDUCE, 1, 1, 2, 1, 1),
+    (GATHER, 1, 1, 4, 0),
+    (GATHER, 1, 1, 4, 1),
+    (REDUCE, 1, 0, 2, 2, 1),
+    (GATHER, 1, 0, 5, 0),
+    (GATHER, 1, 0, 5, 1),
+    (COMPUTE, 1, 0, 1),
+    (TOTAL, 1, 0, 5),
+    (TOTAL, 1, 0, 4),
+    (REDUCE, 1, 1, 2, 2, 0),
+    (REDUCE, 1, 1, 2, 2, 1),
+    (GATHER, 1, 1, 5, 0),
+    (SENT, 1, 0, GATHER),
+    (REDUCE, 1, 0, 5, 1, 0),
+    (GATHER, 1, 1, 5, 1),
+    (REDUCE, 1, 0, 5, 1, 1),
+    (COMPUTE, 1, 1, 1),
+    (TOTAL, 1, 1, 5),
+    (TOTAL, 1, 1, 4),
+    (TOTAL, 1, 0, 3),
+    (SENT, 1, 1, GATHER),
+    (REDUCE, 1, 1, 5, 1, 0),
+    (REDUCE, 1, 1, 5, 1, 1),
+    (TOTAL, 1, 1, 3),
+    (REDUCE, 1, 0, 4, 1, 0),
+    (REDUCE, 1, 0, 4, 1, 1),
+    (REDUCE, 1, 1, 4, 1, 0),
+    (REDUCE, 1, 1, 4, 1, 1),
+    (REDUCE, 1, 0, 5, 2, 0),
+    (REDUCE, 1, 0, 5, 2, 1),
+    (REDUCE, 1, 0, 3, 1, 0),
+    (REDUCE, 1, 1, 5, 2, 0),
+    (REDUCE, 1, 1, 5, 2, 1),
+    (REDUCE, 1, 0, 3, 1, 1),
+    (REDUCE, 1, 0, 4, 2, 0),
+    (REDUCE, 1, 0, 4, 2, 1),
+    (REDUCE, 1, 1, 3, 1, 0),
+    (REDUCE, 1, 1, 3, 1, 1),
+    (REDUCE, 1, 1, 4, 2, 0),
+    (REDUCE, 1, 0, 5, 3, 0),
+    (REDUCE, 1, 1, 4, 2, 1),
+    (REDUCE, 1, 0, 5, 3, 1),
+    (REDUCE, 1, 0, 3, 2, 0),
+    (REDUCE, 1, 1, 5, 3, 0),
+    (REDUCE, 1, 0, 3, 2, 1),
+    (REDUCE, 1, 1, 5, 3, 1),
+    (REDUCE, 1, 1, 3, 2, 0),
+    (REDUCE, 1, 1, 3, 2, 1),
+    (REDUCE, 1, 0, 4, 3, 0),
+    (REDUCE, 1, 0, 4, 3, 1),
+    (REDUCE, 1, 1, 4, 3, 0),
+    (REDUCE, 1, 1, 4, 3, 1),
+    (REDUCE, 1, 0, 3, 3, 0),
+    (REDUCE, 1, 0, 3, 3, 1),
+    (OUTSIDE, 1, 0, 0),
+    (OUTSIDE, 1, 0, 1),
+    (REDUCE, 1, 1, 3, 3, 0),
+    (FINISH, 1, 0, 0),
+    (FINISH, 1, 0, 1),
+    (REDUCE, 1, 1, 3, 3, 1),
+    (SENT, 1, 0, REDUCE),
+    (OUTSIDE, 1, 1, 0),
+    (OUTSIDE, 1, 1, 1),
+    (FINISH, 1, 1, 0),
+    (FINISH, 1, 1, 1),
 )
 
 
@@ -320,18 +398,21 @@
     def place(k):
         return (k % half_rows), pl.ds((k // half_rows) * LANES, LANES)
 
-    def compute(t, s):
-        count = chips * half_rows
-        along = lax.broadcasted_iota(jnp.int32, (count, count), 0)
-        across = lax.broadcasted_iota(jnp.int32, (count, count), 1)
-
-        def turning(inner, outer):
+    def compute(t, s, batch):
+        owners = [(z + chips + k) % chips for k in BATCHES[batch]]
+        count = len(owners) * half_rows
+
+        def turning(shape, inner, outer):
+            along = lax.broadcasted_iota(jnp.int32, shape, 0)
+            across = lax.broadcasted_iota(jnp.int32, shape, 1)
             onehot = across == (along % outer) * inner + along // outer
             return onehot.astype(jnp.float32).astype(jnp.bfloat16)
 
-        folded = held[t, s, :, :, 0:FOLD].reshape(count, FOLD)
+        folded = [held[t, s, chip, :, 0:FOLD] for chip in owners]
         turned = jnp.dot(
-            turning(half_rows, chips), folded, preferred_element_type=jnp.float32
+            turning((chips * half_rows, count), half_rows, chips),
+            jnp.concatenate(folded, axis=0),
+            preferred_element_type=jnp.float32,
         )
         for k in range(folds):
             row, lanes = place(k)
@@ -339,11 +420,17 @@
             extra_in[0:chips, k * LANES : (k + 1) * LANES] = turned[
                 row * chips : (row + 1) * chips, start : start + LANES
             ]
-        tokens = held[t, s, :, :, FOLD : FOLD + width].reshape(count, width)
-        tokens = jnp.concatenate([tokens, extra_in[...].astype(jnp.bfloat16)], axis=0)
+        tokens = [held[t, s, chip, :, FOLD : FOLD + width] for chip in owners]
+        tokens = jnp.concatenate(tokens + [extra_in[...].astype(jnp.bfloat16)], axis=0)
         acts = jnp.dot(tokens, both[...], preferred_element_type=jnp.float32)
         gate_act, up_act = acts[:, : 2 * units], acts[:, 2 * units :]
         hidden = (gate_act * jax.nn.sigmoid(gate_act) * up_act).astype(jnp.bfloat16)
+
+        def put_out(values, cols):
+            values = values.astype(jnp.bfloat16)
+            for i, chip in enumerate(owners):
+                part[t, s, chip, :, cols] = values[i * half_rows : (i + 1) * half_rows]
+
         step = 2 * LANES
         for start in range(0, width, step):
             product = jnp.dot(
@@ -355,14 +442,13 @@
                 extra_out[row * chips : (row + 1) * chips, lanes] = product[
                     count : count + chips, at : at + LANES
                 ]
-            product = product[:count].astype(jnp.bfloat16).reshape(chips, half_rows, step)
-            part[t, s, :, :, pl.ds(FOLD + start, step)] = product
+            put_out(product, pl.ds(FOLD + start, step))
         folded = jnp.dot(
-            turning(chips, half_rows),
+            turning((count, chips * half_rows), chips, half_rows),
             extra_out[...].astype(jnp.bfloat16),
             preferred_element_type=jnp.float32,
         )
-        part[t, s, :, :, 0:FOLD] = folded.astype(jnp.bfloat16).reshape(chips, half_rows, FOLD)
+        put_out(folded, pl.ds(0, FOLD))
 
     def reduce_copy(t, s, way, d, h, dst, index, device):
         return remote(
@@ -394,31 +480,23 @@
                 for h in range(PIECES):
                     reduce_on(t, s, way, d, h).start()
 
-    def reduce_step(t, s, r, h):
-        d = REACH - r
+    def reduce_step(t, s, start, hop, h):
+        d = start - hop
         for way, rank in enumerate(ranks):
 
-            @pl.when((rank >= d - 2) & (rank < group - 1))
+            @pl.when(rank == group - 1 - hop)
             def _():
                 reduce_on(t, s, way, d + 1, h).wait_recv()
                 if d >= 1:
                     add_up(t, s, way, d, h)
-
-                    @pl.when(rank >= 1)
-                    def _():
-                        reduce_on(t, s, way, d, h).start()
-
-                    if d <= 2:
-
-                        @pl.when(rank == 0)
-                        def _():
-                            reduce_out(t, s, way, d, h).start()
-
-            if d == 0:
-
-                @pl.when(rank >= group - 2)
-                def _():
-                    reduce_out(t, s, way, 1, h).wait_recv()
+                    (reduce_on if hop < group - 1 else reduce_out)(t, s, way, d, h).start()
+
+    def reduce_outside(t, s, h):
+        for way, rank in enumerate(ranks):
+
+            @pl.when(rank >= group - 2)
+            def _():
+                reduce_out(t, s, way, 1, h).wait_recv()
 
     def finish_reduce(t, s):
         for h in range(PIECES):
@@ -557,53 +635,62 @@
     for load in loads:
         load.start()
     fold[...] = jnp.zeros_like(fold)
-    extra_in[...] = jnp.zeros_like(extra_in)
-    extra_out[...] = jnp.zeros_like(extra_out)
-    for way, rank in enumerate(ranks):
-
-        @pl.when(rank == group - 1)
-        def _():
-            for t in range(2):
-                for s in range(2):
-                    sums[way, t, s, 0] = jnp.zeros_like(sums[way, t, s, 0])
+    def clear():
+        extra_in[...] = jnp.zeros_like(extra_in)
+        extra_out[...] = jnp.zeros_like(extra_out)
+        for way, rank in enumerate(ranks):
+
+            @pl.when(rank == group - 1)
+            def _():
+                for t0 in range(2):
+                    for s0 in range(2):
+                        sums[way, t0, s0, 0] = jnp.zeros_like(sums[way, t0, s0, 0])
 
     entered = []
     for step, t, s, *at in ORDER:
-        if step == "prepare":
+        if step == PREPARE:
             if t == 0:
                 current[s] = states[s][0]
             else:
                 receive(s)
             prepare(t, s)
-        elif step == "start":
+        elif step == START:
             if not entered:
                 pl.semaphore_wait(barrier, len(partners))
             start_gather(t, s)
             if not entered:
                 for copy in share_copies():
                     copy.start()
+                clear()
             entered.append(step)
-        elif step == "gather":
+        elif step == GATHER:
             gather_step(t, s, *at)
-        elif step == "compute":
-            if (t, s) == (0, 0):
+        elif step == COMPUTE:
+            if (t, s, *at) == (0, 0, 0):
                 for load in loads:
                     load.wait()
                 for copy in share_copies():
                     copy.wait()
-            compute(t, s)
-        elif step == "total":
+            compute(t, s, *at)
+        elif step == SENT:
+            (finish_gather if at[0] == GATHER else finish_reduce)(t, s)
+        elif step == TOTAL:
             start_reduce(t, s, *at)
-        elif step == "reduce":
+        elif step == REDUCE:
             reduce_step(t, s, *at)
+        elif step == OUTSIDE:
+            reduce_outside(t, s, *at)
         else:
             finalize(t, s, *at)
+    finish_reduce(1, 1)
     for s in range(2):
-        for t in range(2):
-            finish_gather(t, s)
-            finish_reduce(t, s)
         for h in range(PIECES):
             pipe_copy(s, h).wait_send()
+
+
+def hand_over(first, second, first_out, second_out):
+    first_out[:, 0] = first[...]
+    second_out[:, 0] = second[...]
 
 
 def shards(
@@ -673,7 +760,14 @@
         first_routes.reshape(steps, 1, rows),
         second_routes.reshape(steps, 1, rows),
     )
-    return (outs[0][:, None], outs[1][:, None])
+    whole = jax.ShapeDtypeStruct((steps, 1, rows, width), bf16)
+    return pl.pallas_call(
+        hand_over,
+        out_shape=(whole, whole),
+        in_specs=[vmem] * 2,
+        out_specs=(vmem, vmem),
+        name="hand_over",
+    )(*outs)
 
 
 def solution(mesh):

time: 146 us -> 138 us (0.945)
  Pallas kernels: 143 us -> 137 us
  local copies, waits for them, and re-layouts: 2.64 us -> 0 us
    pallas_call x1, Pallas kernels: 143 us -> 135 us  [shards(): pl.pallas_call(functools.partial(relay_kernel, chips, sections), out_shap...]
    unnamed x4 -> x0, local copies, waits for them, and re-layouts: 2.64 us -> none
    pallas_call x0 -> x1, Pallas kernels: none -> 2.11 us  [shards(): pl.pallas_call(hand_over, out_shape=(whole, whole), in_specs=[vmem] * 2,...]
where the time goes in v4:
time: 138 us; the launch traced here: 137 us
  Pallas kernels  137 us (99%)
    pallas_call x1, Pallas kernels, shards(): pl.pallas_call(functools.partial(relay_kernel, chips, sections), out_shap...  135 us

profile of v4, /device:TPU:6, one launch (start us, length us, event | category | flops | bytes accessed | tf_op | source)
XLA Modules:
  0.0 137.3 jit_solution(1144266809010560833)
XLA Ops:
  0.6 134.6 %relay_window.1 = (bf16[2,32,3584]{2,1,0:T(8,128)(2,1)}, bf16[2,32,3584]{2,1,0:T(8,128)(2,1)}) custom-call(bf16[1,32,3584]{2,1,0:T(8,128)(2,1)} %first_state.1, bf16[1,32,3584]{2,1,0:T(8,128)(2,1)} %second_state.1, bf16[1,32,3584]{2,1,0:T(8,128)(2,1)} %first_enter.1, bf16[1,32,3584]{2,1,0:T(8,128)(2,1)} %second_enter.1, f32[1,3584]{1,0:T(1,128)} %gains.1, ...), custom_call_target="tpu_custom_call" | custom-call | tf_op jit(solution)/shard_map/relay_window/pallas_call | solution.py:720
  135.2 2.1 %hand_over.1 = (bf16[2,1,32,3584]{3,2,1,0:T(8,128)(2,1)}, bf16[2,1,32,3584]{3,2,1,0:T(8,128)(2,1)}) custom-call(bf16[2,32,3584]{2,1,0:T(8,128)(2,1)} %get-tuple-element.4.first, bf16[2,32,3584]{2,1,0:T(8,128)(2,1)} %get-tuple-element.5.second), custom_call_target="tpu_custom_call" | custom-call | tf_op jit(solution)/shard_map/hand_over/pallas_call | solution.py:764

commit v5 on v4

--- a/solution.py
+++ b/solution.py
@@ -100,8 +100,8 @@
     (REDUCE, 0, 1, 5, 2, 1),
     (REDUCE, 0, 0, 3, 3, 1),
     (OUTSIDE, 0, 0, 0),
+    (FINISH, 0, 0, 0),
     (OUTSIDE, 0, 0, 1),
-    (FINISH, 0, 0, 0),
     (REDUCE, 0, 1, 3, 1, 0),
     (REDUCE, 0, 1, 3, 1, 1),
     (REDUCE, 0, 1, 4, 2, 0),
@@ -212,11 +212,11 @@
     (REDUCE, 1, 1, 3, 3, 0),
     (FINISH, 1, 0, 0),
     (FINISH, 1, 0, 1),
+    (OUTSIDE, 1, 1, 0),
+    (FINISH, 1, 1, 0),
+    (SENT, 1, 0, REDUCE),
     (REDUCE, 1, 1, 3, 3, 1),
-    (SENT, 1, 0, REDUCE),
-    (OUTSIDE, 1, 1, 0),
     (OUTSIDE, 1, 1, 1),
-    (FINISH, 1, 1, 0),
     (FINISH, 1, 1, 1),
 )
 
@@ -689,8 +689,8 @@
 
 
 def hand_over(first, second, first_out, second_out):
-    first_out[:, 0] = first[...]
-    second_out[:, 0] = second[...]
+    first_out[0] = first[...]
+    second_out[0] = second[...]
 
 
 def shards(
@@ -761,11 +761,14 @@
         second_routes.reshape(steps, 1, rows),
     )
     whole = jax.ShapeDtypeStruct((steps, 1, rows, width), bf16)
+    given = pl.BlockSpec((1, rows, width), lambda step: (step, 0, 0))
+    result = pl.BlockSpec((1, 1, rows, width), lambda step: (step, 0, 0, 0))
     return pl.pallas_call(
         hand_over,
+        grid=(steps,),
         out_shape=(whole, whole),
-        in_specs=[vmem] * 2,
-        out_specs=(vmem, vmem),
+        in_specs=[given] * 2,
+        out_specs=(result, result),
         name="hand_over",
     )(*outs)
 

time: 138 us -> 138 us (level)
  no operation moved by 1% of the time
where the time goes in v5:
time: 138 us; the launch traced here: 137 us
  Pallas kernels  137 us (99%)
    pallas_call x1, Pallas kernels, shards(): pl.pallas_call(functools.partial(relay_kernel, chips, sections), out_shap...  135 us

profile of v5, /device:TPU:6, one launch (start us, length us, event | category | flops | bytes accessed | tf_op | source)
XLA Modules:
  0.0 137.4 jit_solution(5486681950252334068)
XLA Ops:
  0.6 134.7 %relay_window.1 = (bf16[2,32,3584]{2,1,0:T(8,128)(2,1)}, bf16[2,32,3584]{2,1,0:T(8,128)(2,1)}) custom-call(bf16[1,32,3584]{2,1,0:T(8,128)(2,1)} %first_state.1, bf16[1,32,3584]{2,1,0:T(8,128)(2,1)} %second_state.1, bf16[1,32,3584]{2,1,0:T(8,128)(2,1)} %first_enter.1, bf16[1,32,3584]{2,1,0:T(8,128)(2,1)} %second_enter.1, f32[1,3584]{1,0:T(1,128)} %gains.1, ...), custom_call_target="tpu_custom_call" | custom-call | tf_op jit(solution)/shard_map/relay_window/pallas_call | solution.py:720
  135.4 2.1 %hand_over.1 = (bf16[2,1,32,3584]{3,2,1,0:T(8,128)(2,1)}, bf16[2,1,32,3584]{3,2,1,0:T(8,128)(2,1)}) custom-call(bf16[2,32,3584]{2,1,0:T(8,128)(2,1)} %get-tuple-element.4.first, bf16[2,32,3584]{2,1,0:T(8,128)(2,1)} %get-tuple-element.5.second), custom_call_target="tpu_custom_call" | custom-call | tf_op jit(solution)/shard_map/hand_over/pallas_call | solution.py:766
